TPU v7x, 128 devices: a whole 4x4x4 slice. The times are simulated.
128 devices in a mesh: blk: 8 (over y, x_hi), grp: 16 (over x_lo, z, core).
Axes of the slice: x: 4 (x_hi: 2, x_lo: 2; x = x_hi * 2 + x_lo), y: 4, z: 4, core: 2. Of those that a mesh axis runs over, the one named last changes fastest.
Arguments:
- grad_out: bfloat16 [16, 32768, 256], P('grp', 'blk'), may hold values from -6 to 6
- pre_act: bfloat16 [16, 32768, 256], P('grp', 'blk'), may hold values from -6 to 6
- node_feats: bfloat16 [16, 32768, 256], P('grp', 'blk'), may hold values from -6 to 6
- w_message: bfloat16 [256, 256], replicated, may hold values from -0.375 to 0.375
- w_update: bfloat16 [256, 256], replicated, may hold values from -0.375 to 0.375
- tile_vals: bfloat16 [16, 8, 8, 16, 128, 128], P('grp', 'blk'), may hold values from -0.25 to 0.25
- tile_rows: int32 [16, 8, 8, 16], P('grp'), may hold values from 0 to 31
- tile_cols: int32 [16, 8, 8, 16], P('grp', 'blk'), may hold values from 0 to 31
- rec_slab: int32 [16, 32768, 1], P('grp', 'blk'), may hold values from 0 to 15; in each aligned block of 4096 rows (0 to 4095, 4096 to 8191, ..., all dimensions but the last counted through in order) at most 512 rows name the same one
- rec_local: int32 [16, 32768], P('grp', 'blk'), may hold values from 0 to 4095
- rec_remote: int32 [16, 32768], P('grp', 'blk'), may hold values from 0 to 4095
- rec_weight: float32 [16, 32768], P('grp', 'blk'), may hold values from 0.25 to 2
Outputs:
- grad_feats: bfloat16 [16, 32768, 256], P('grp', 'blk')
- grad_message: float32 [256, 256], replicated
- grad_update: float32 [256, 256], replicated
Inputs may be any that keep to these rules, and one draw needn't show every extreme that they name: `rec_slab`: among the 4096 records of one device at most 512 name the same slab, and in every draw some device has a slab named by exactly 512 of its records.
All inputs are finite; a program needn't handle non-finite values.
Results may differ from a plain program's by a relative error of at most 0.009.
Values may be sent and summed in bfloat16 or wider, within the bound.
A program may use at most 128 MiB of HBM per device.

v0:
```python
import jax
import jax.numpy as jnp
from jax import lax
from jax.sharding import PartitionSpec as P


def silu_slope(value):
    sig = jax.nn.sigmoid(value)
    return sig * (1.0 + value * (1.0 - sig))


def local(
    grad_out,
    pre_act,
    node_feats,
    w_message,
    w_update,
    tile_vals,
    tile_rows,
    tile_cols,
    rec_slab,
    rec_local,
    rec_remote,
    rec_weight,
):
    grad = grad_out[0]
    rows = grad.shape[0]
    width = grad.shape[1]
    slabs = lax.axis_size("grp")
    parts = lax.axis_size("blk")
    mine = lax.axis_index("blk")
    records = rec_local.shape[1]
    capacity = 2 * records // slabs
    dest = rec_slab[0, :, 0]
    choose = (dest[:, None] == jnp.arange(slabs, dtype=jnp.int32)[None, :]).astype(jnp.int32)
    before = jnp.sum((jnp.cumsum(choose, axis=0) - choose) * choose, axis=1)
    placed = dest * capacity + before
    picked = grad[rec_local[0]].astype(jnp.float32)
    payload = (rec_weight[0][:, None] * picked).astype(jnp.bfloat16)
    outgoing = jnp.zeros((slabs * capacity, width), jnp.bfloat16).at[placed].set(payload)
    target = jnp.full((slabs * capacity,), rows, jnp.int32).at[placed].set(rec_remote[0])
    upper = (target // 64).astype(jnp.float32).astype(jnp.bfloat16).reshape(slabs, capacity)
    lower = (target % 64).astype(jnp.float32).astype(jnp.bfloat16).reshape(slabs, capacity)
    arrived, got_upper, got_lower = (
        lax.all_to_all(
            outgoing.reshape(slabs, capacity, width), "grp", split_axis=0, concat_axis=0, tiled=True
        ),
        lax.all_to_all(upper, "grp", split_axis=0, concat_axis=0, tiled=True),
        lax.all_to_all(lower, "grp", split_axis=0, concat_axis=0, tiled=True),
    )
    landing = (
        (got_upper.astype(jnp.float32) * 64.0 + got_lower.astype(jnp.float32))
        .astype(jnp.int32)
        .reshape(-1)
    )
    grad_h = (
        grad.astype(jnp.float32)
        .at[landing]
        .add(arrived.reshape(-1, width).astype(jnp.float32), mode="drop")
        .astype(jnp.bfloat16)
    )
    pre = pre_act[0].astype(jnp.float32)
    act = jax.nn.silu(pre).astype(jnp.bfloat16)
    upd_term = jnp.einsum("nd,ne->de", act, grad_h, preferred_element_type=jnp.float32)
    scale = 1.0 / jnp.sqrt(jnp.float32(slabs * parts * rows))
    grad_update = lax.psum(upd_term, ("blk", "grp")) * scale
    back = jnp.einsum("ne,de->nd", grad_h, w_update, preferred_element_type=jnp.float32)
    grad_pre = (back * silu_slope(pre)).astype(jnp.bfloat16)
    tiles = tile_vals[0, 0]
    tile = tiles.shape[-1]
    blocks = rows // tile
    my_rows = lax.dynamic_index_in_dim(tile_rows[0], mine, 0, False)
    my_cols = tile_cols[0, 0]
    total = jnp.zeros((blocks, tile, width), jnp.float32)
    piece = lax.all_gather(grad_pre, "blk", axis=0, tiled=True)
    start = jnp.int32(0)
    count = piece.shape[0] // rows
    for offset in range(count):
        owner = start // rows + offset
        panel = piece[offset * rows : (offset + 1) * rows].reshape(blocks, tile, width)
        tiles_here = lax.dynamic_index_in_dim(tiles, owner, 0, False)
        rows_here = lax.dynamic_index_in_dim(my_rows, owner, 0, False)
        cols_here = lax.dynamic_index_in_dim(my_cols, owner, 0, False)
        chosen = panel[rows_here]
        contrib = jnp.einsum("tij,tid->tjd", tiles_here, chosen, preferred_element_type=jnp.float32)
        total = total.at[cols_here].add(contrib)
    spread = total.reshape(rows, width).astype(jnp.bfloat16)
    msg_term = jnp.einsum("nd,ne->de", node_feats[0], spread, preferred_element_type=jnp.float32)
    grad_feats = (
        grad_h.astype(jnp.float32)
        + jnp.einsum("ne,de->nd", spread, w_message, preferred_element_type=jnp.float32)
    ).astype(jnp.bfloat16)
    grad_message = lax.psum(msg_term, ("blk", "grp")) * scale
    return (grad_feats[None], grad_message, grad_update)


def solution(mesh):
    placed = (
        P("grp", "blk", None),
        P("grp", "blk", None),
        P("grp", "blk", None),
        P(),
        P(),
        P("grp", "blk", None, None, None, None),
        P("grp", None, None, None),
        P("grp", "blk", None, None),
        P("grp", "blk", None),
        P("grp", "blk"),
        P("grp", "blk"),
        P("grp", "blk"),
    )
    return jax.shard_map(
        local,
        mesh=mesh,
        in_specs=placed,
        out_specs=(P("grp", "blk", None), P(), P()),
        check_vma=False,
    )
```

profile of v0, /device:TPU:1, one launch (start us, length us, event | category | flops | bytes accessed | tf_op | source)
XLA Modules:
  0.0 685.1 jit_solution(11151744121443705415)
XLA Ops:
  7.2 0.9 fusion.40
  8.1 4.6 reduce-window.6
  13.5 0.9 fusion.39
  14.4 0.7 compare_select_fusion.2
  15.2 15.7 %scatter_custom_fusion = s32[8192]{0:T(1024)S(1)} fusion(s32[4096]{0:T(1024)S(1)} %bitcast.230, s32[4096]{0:T(1024)} %bitcast.232, s32[]{:T(128)} %constant.367.clone.1), kind=kCustom, calls=%fused_computation.96 | custom fusion | bytes 33280 | tf_op jit(solution)/shard_map/scatter | solution.py:41
  31.5 0.7 reduce.2
  32.2 0.6 reshape.855
  32.8 7.8 %all-to-all-start.1 = ((bf16[16,2,256]{2,1,0:T(2,128)(2,1)}), bf16[16,2,256]{2,1,0:T(2,128)(2,1)S(1)}, u32[]{:S(2)}, u32[]{:S(2)}) async-start(bf16[16,2,256]{2,1,0:T(2,128)(2,1)} %reshape.855), calls=%async_computation.1 | async-start | bytes 32768 | tf_op jit(solution)/shard_map/all_to_all | solution.py:49
  40.7 0.7 reduce.3
  41.4 0.6 reshape.857
  42.0 4.4 all-to-all-done.1
  46.4 3.7 all-to-all-start
  50.1 48.8 %scatter_custom_fusion.1 = bf16[8192,256]{1,0:T(8,128)(2,1)} fusion(s32[4096]{0:T(1024)S(1)} %bitcast.231, f32[4096]{0:T(1024)S(1)} %bitcast.229, bf16[]{:T(256)} %constant.377.clone.1, bf16[4096,256]{1,0:T(8,128)(2,1)} %bitcast.210, s32[4096]{0:T(1024)S(1)} %broadcast_clamp_fusion), kind=kCustom, calls=%fused_computation.37 | custom fusion | flops 3145728 | bytes 6324226 | tf_op jit(solution)/shard_map/scatter | solution.py:40
  98.9 5.8 all-to-all-start.2
  104.9 3.8 bitcast_convert_fusion
  108.9 51.5 %all-to-all-done.2 = bf16[16,512,256]{2,1,0:T(8,128)(2,1)} async-done(((bf16[16,512,256]{2,1,0:T(8,128)(2,1)}), bf16[16,512,256]{2,1,0:T(8,128)(2,1)}, u32[]{:S(2)}, u32[]{:S(2)}) %all-to-all-start.2) | async-done | bytes 4194336 | tf_op jit(solution)/shard_map/all_to_all | solution.py:45
  160.3 49.2 %scatter_custom_fusion.2 = f32[4096,256]{1,0:T(8,128)} fusion(f32[4096,256]{1,0:T(8,128)} %bitcast_convert_fusion, s32[8192]{0:T(1024)S(1)} %bitcast.228, bf16[8192,256]{1,0:T(8,128)(2,1)} %bitcast.77), kind=kCustom, calls=%fused_computation.20 | custom fusion | flops 4194304 | bytes 8388608 | tf_op jit(solution)/shard_map/scatter-add | solution.py:59
  209.5 6.0 fusion.2
  216.2 1.0 fusion.64
  217.3 5.1 fusion.16
  222.4 182.2 %all-gather.2.cloned.1.call-done = bf16[32768,256]{1,0:T(8,128)(2,1)} async-done(((bf16[4096,256]{1,0:T(8,128)(2,1)}), bf16[32768,256]{1,0:T(8,128)(2,1)}) %all-gather.2.cloned.1.call-update) | async-done | bytes 16777232 | tf_op jit(solution)/shard_map/all_gather | solution.py:75
  404.5 12.3 %fusion.77 = (bf16[4096,256]{1,0:T(8,128)(2,1)}, bf16[4096,256]{1,0:T(8,128)(2,1)}, bf16[4096,256]{1,0:T(8,128)(2,1)}, bf16[4096,256]{1,0:T(8,128)(2,1)}, bf16[4...) fusion(bf16[32768,256]{1,0:T(8,128)(2,1)} %all-gather.2.cloned.1.cal, ...), kind=kLoop, calls=%fused_computation.160 | loop fusion | bytes 33554432 | tf_op jit(solution)/shard_map/slice | solution.py:80
  416.9 2.2 gather_fusion
  419.1 2.9 convolution_bitcast_fusion.7
  422.0 2.9 copy.48
  424.9 2.2 gather_fusion.1
  427.1 2.9 convolution_bitcast_fusion.6
  430.0 2.9 copy.50
  432.9 2.2 gather_fusion.2
  435.1 2.9 convolution_bitcast_fusion.5
  438.0 3.0 copy.52
  440.9 2.2 gather_fusion.3
  443.1 2.9 convolution_bitcast_fusion.4
  446.0 2.9 copy.54
  448.9 2.2 gather_fusion.4
  451.1 2.9 convolution_bitcast_fusion.3
  454.0 2.9 copy.56
  456.9 2.2 gather_fusion.5
  459.1 2.9 convolution_bitcast_fusion.2
  462.0 2.9 copy.58
  464.9 2.2 gather_fusion.6
  467.1 2.9 convolution_bitcast_fusion.1
  470.0 2.9 copy.60
  472.9 2.2 gather_fusion.7
  475.1 2.8 convolution_bitcast_fusion
  477.9 2.9 copy.62
  480.8 2.4 broadcast_in_dim.7
  483.3 5.2 scatter_fusion
  488.4 5.2 scatter_fusion.1
  493.6 5.2 scatter_fusion.2
  498.8 5.6 scatter_fusion.3
  504.4 5.2 scatter_fusion.4
  509.7 5.2 scatter_fusion.5
  514.9 5.1 scatter_fusion.6
  520.0 5.2 scatter_fusion.7
  525.2 2.5 convert_element_type.120
  527.7 1.3 copy-done.1
  529.1 1.4 fusion.18
  530.6 4.9 fusion.4
  535.4 139.2 %all-reduce.3.cloned.1.call-done = (f32[256,256]{0,1:T(8,128)}, f32[256,256]{0,1:T(8,128)}) async-done(((f32[256,256]{0,1:T(8,128)}, f32[256,256]{0,1:T(8,128)}), (f32[256,256]{0,1:T(8,128)}, f32[256,256]{0,1:T(8,128)})) %all-reduce.3.cloned.1.call-update) | async-done | bytes 524304 | tf_op jit(solution)/shard_map/psum | solution.py:93
  674.7 1.0 broadcast_multiply_fusion.1
  675.6 0.8 copy.64
  676.5 1.0 broadcast_multiply_fusion
  677.5 0.8 copy.65
  (39 shorter events, 2.5 us)
Async XLA Ops:
  7.2 521.9 %copy-start = (bf16[1,4096,256]{2,1,0:T(8,128)(2,1)S(1)}, bf16[1,4096,256]{2,1,0:T(8,128)(2,1)}, u32[]{:S(2)}) copy-start(bf16[1,4096,256]{2,1,0:T(8,128)(2,1)} %param.14) | copy-start | bytes 6291460
  7.2 33.4 %copy-start.4 = (s32[1,4096]{1,0:T(1,128)S(1)}, s32[1,4096]{1,0:T(1,128)}, u32[]{:S(2)}) copy-start(s32[1,4096]{1,0:T(1,128)} %param.21) | copy-start | bytes 49156
  7.2 42.9 %copy-start.3 = (f32[1,4096]{1,0:T(1,128)S(1)}, f32[1,4096]{1,0:T(1,128)}, u32[]{:S(2)}) copy-start(f32[1,4096]{1,0:T(1,128)} %param.23) | copy-start | bytes 49156
  32.8 13.5 %all-to-all-start.1 = ((bf16[16,2,256]{2,1,0:T(2,128)(2,1)}), bf16[16,2,256]{2,1,0:T(2,128)(2,1)S(1)}, u32[]{:S(2)}, u32[]{:S(2)}) async-start(bf16[16,2,256]{2,1,0:T(2,128)(2,1)} %reshape.855), calls=%async_computation.1 | async-start | bytes 32768 | tf_op jit(solution)/shard_map/all_to_all | solution.py:49
  46.4 52.5 %all-to-all-start = ((bf16[16,2,256]{2,1,0:T(2,128)(2,1)}), bf16[16,2,256]{2,1,0:T(2,128)(2,1)S(1)}, u32[]{:S(2)}, u32[]{:S(2)}) async-start(bf16[16,2,256]{2,1,0:T(2,128)(2,1)} %reshape.857), calls=%async_computation | async-start | bytes 32768 | tf_op jit(solution)/shard_map/all_to_all | solution.py:48
  98.9 61.5 %all-to-all-start.2 = ((bf16[16,512,256]{2,1,0:T(8,128)(2,1)}), bf16[16,512,256]{2,1,0:T(8,128)(2,1)}, u32[]{:S(2)}, u32[]{:S(2)}) async-start(bf16[16,512,256]{2,1,0:T(8,128)(2,1)} %bitcast.209), calls=%async_computation.2 | async-start | bytes 8388608 | tf_op jit(solution)/shard_map/all_to_all | solution.py:45
  104.6 299.9 %all-gather.2.cloned.1.call-start = ((), (), s32[]{:S(2)}) async-start(), calls=%async_computation.3 | async-start | bytes 18874368 | tf_op jit(solution)/shard_map/all_gather | solution.py:75
  160.3 49.2 %copy-start.6 = (bf16[256,256]{1,0:T(8,128)(2,1)S(1)}, bf16[256,256]{1,0:T(8,128)(2,1)}, u32[]{:S(2)}) copy-start(bf16[256,256]{1,0:T(8,128)(2,1)} %param.16) | copy-start | bytes 393220
  215.5 0.7 copy-start.5
  215.5 459.1 %all-reduce.3.cloned.1.call-start = ((), (), s32[]{:S(2)}) async-start(), calls=%async_computation.4 | async-start | bytes 1048576 | tf_op jit(solution)/shard_map/psum | solution.py:93
  527.7 1.4 copy-start.1
  529.1 1.5 copy-start.2
Sparse Core Ops, SparseCore 0:
  215.7 188.8 all-gather.1
  530.7 143.9 all-reduce.2
where the time goes:
time: 687 us; the launch traced here: 685 us
  waiting for transfers between devices  377 us (55%)
  other arithmetic  158 us (23%)
  local copies, waits for them, and re-layouts  77.3 us (11%)
  matrix products  40.3 us (6%)
  starting transfers between devices  17.5 us (3%)
  between operations  14.4 us (2%)
    all_gather x1, waiting for transfers between devices, local(): piece = lax.all_gather(grad_pre, 'blk', axis=0, tiled=True)  182 us
    psum x1, waiting for transfers between devices, local(): grad_message = lax.psum(msg_term, ('blk', 'grp')) * scale  139 us
    all_to_all x1, waiting for transfers between devices, local(): lax.all_to_all(outgoing.reshape(slabs, capacity, width), 'grp', split_axi...  51.5 us
    scatter-add x1, other arithmetic, local(): grad_h = grad.astype(jnp.float32).at[landing].add(arrived.reshape(-1, wid...  49.2 us
    scatter x1, other arithmetic, local(): jnp.zeros((slabs * capacity, width), jnp.bfloat16).at[placed].set(payload)  48.8 us
    scatter-add x8, other arithmetic, local(): total = total.at[cols_here].add(contrib)  42 us
    dot_general x8, local copies, waits for them, and re-layouts, local(): jnp.einsum('tij,tid->tjd', tiles_here, chosen, preferred_element_type=jnp...  23.3 us
    dot_general x8, matrix products, local(): jnp.einsum('tij,tid->tjd', tiles_here, chosen, preferred_element_type=jnp...  23 us
  transfers between devices with their start and end apart: 5, of which 4 were waited for; matrix products, arithmetic and copies ran while one was open for 10% of the time, Pallas kernels for 0%

commit v1 on v0

v1 whole, which is shorter than its diff:
```python
import functools

import jax
import jax.numpy as jnp
from jax import lax
from jax.experimental import pallas as pl
from jax.experimental.pallas import tpu as pltpu
from jax.sharding import PartitionSpec as P

F32 = jnp.float32
BF16 = jnp.bfloat16
MESH = pl.DeviceIdType.MESH
NT = (((1,), (1,)), ((), ()))
TN = (((0,), (0,)), ((), ()))
EXT = 16
VMEM_LIMIT = 56 * 1024 * 1024


def iota(shape, dim):
    return lax.broadcasted_iota(jnp.int32, shape, dim)


def prep_kernel(slab_ref, local_ref, remote_ref, weight_ref, grad_ref, out_ref, node_ref, scale_ref, ext_ref):
    slabs, cap = node_ref.shape[0], node_ref.shape[1]
    chunks = slab_ref.shape[0]
    nodes = grad_ref.shape[0]

    @pl.when(pl.program_id(0) == 0)
    def _():
        slab = slab_ref[...]
        ids = iota((chunks, slabs, 128), 1)
        choose = jnp.where(ids == slab[:, None, :], 1.0, 0.0)
        flat = choose.reshape(chunks * slabs, 128)
        flat16 = flat.astype(BF16)
        upper = jnp.where(iota((128, 128), 0) < iota((128, 128), 1), 1.0, 0.0).astype(BF16)
        prefix = jnp.dot(flat16, upper, preferred_element_type=F32)
        totals = jnp.dot(flat16, jnp.ones((128, 128), BF16), preferred_element_type=F32)
        size = chunks * slabs
        row, col = iota((size, size), 0), iota((size, size), 1)
        earlier = (col < row) & (lax.rem(col, slabs) == lax.rem(row, slabs))
        offset = jnp.dot(jnp.where(earlier, 1.0, 0.0).astype(BF16), totals.astype(BF16), preferred_element_type=F32)
        place = ((prefix + offset) * flat).reshape(chunks, slabs, 128).sum(axis=1).astype(jnp.int32)
        remote, local, weight = remote_ref[...], local_ref[...], weight_ref[...]
        first = weight.astype(BF16).astype(F32)
        second = (weight - first).astype(BF16).astype(F32)
        third = weight - first - second
        values = [
            (remote // 64).astype(F32),
            (remote % 64).astype(F32),
            (local // 64).astype(F32),
            (local % 64).astype(F32),
            first,
            second,
            third,
            jnp.ones_like(weight),
        ]
        table = jnp.zeros((len(values) * slabs, cap), F32)
        for c in range(chunks):
            left = jnp.concatenate([choose[c] * v[c : c + 1] for v in values], axis=0).astype(BF16)
            right = jnp.where(iota((cap, 128), 0) == place[c : c + 1], 1.0, 0.0).astype(BF16)
            table += lax.dot_general(left, right, NT, preferred_element_type=F32)
        valid = table[7 * slabs : 8 * slabs]
        upper_part = jnp.where(valid > 0.5, table[:slabs], 64.0)
        lower_part = table[slabs : 2 * slabs]
        half = cap // 2
        for s in range(slabs):
            rows = [part[s : s + 1, q * half : (q + 1) * half] for part in (upper_part, lower_part) for q in range(2)]
            block = jnp.concatenate(rows + [jnp.zeros((EXT - 4, half), F32)], axis=0)
            ext_ref[s] = block.astype(BF16)
        turned = jnp.transpose(table)
        for s in range(slabs):
            at = lambda v: turned[:, v * slabs + s : v * slabs + s + 1]
            node_ref[s] = jnp.broadcast_to((at(2) * 64.0 + at(3)).astype(jnp.int32), (cap, 128))
            scale_ref[s] = jnp.broadcast_to(at(4) + at(5) + at(6), (cap, 128))

    s = pl.program_id(0)
    wide = 1024
    node = node_ref[s]
    lane = iota((cap, 128), 1)
    total = jnp.zeros((cap, grad_ref.shape[1]), F32)
    for k in range(nodes // wide):
        pieces = [
            jnp.where(node == lane + (k * wide + j * 128), 1.0, 0.0).astype(BF16) for j in range(wide // 128)
        ]
        total += jnp.dot(
            jnp.concatenate(pieces, axis=1), grad_ref[k * wide : (k + 1) * wide], preferred_element_type=F32
        )
    scale = scale_ref[s]
    out_ref[0, :cap] = (total * jnp.concatenate([scale, scale], axis=1)).astype(BF16)
    out_ref[0, cap:] = ext_ref[s]


def prep(slab, local, remote, weight, grad, slabs, cap):
    nodes, width = grad.shape
    whole = lambda a: pl.BlockSpec(a.shape, lambda i: (0,) * a.ndim)
    args = (slab, local, remote, weight, grad)
    return pl.pallas_call(
        prep_kernel,
        grid=(slabs,),
        out_shape=jax.ShapeDtypeStruct((slabs, cap + EXT, width), BF16),
        in_specs=[whole(a) for a in args],
        out_specs=pl.BlockSpec((1, cap + EXT, width), lambda i: (i, 0, 0)),
        scratch_shapes=[
            pltpu.VMEM((slabs, cap, 128), jnp.int32),
            pltpu.VMEM((slabs, cap, 128), F32),
            pltpu.VMEM((slabs, EXT, width), BF16),
        ],
        compiler_params=pltpu.CompilerParams(vmem_limit_bytes=VMEM_LIMIT),
        name="prep",
    )(*args)


def node_kernel(
    picks_ref, arrived_ref, grad_ref, pre_ref, w_ref, gradh_ref, upd_ref, packed_ref, target_ref, gp_ref, sem
):
    slabs, cap = arrived_ref.shape[0], arrived_ref.shape[1] - EXT
    parts, picks = packed_ref.shape[0], packed_ref.shape[1]
    half = cap // 2
    tall = grad_ref.shape[0]
    i = pl.program_id(0)

    @pl.when(i == 0)
    def _():
        upd_ref[...] = jnp.zeros_like(upd_ref)
        for s in range(slabs):
            ext = arrived_ref[s, cap:].astype(F32)
            target_ref[s : s + 1, :half] = (ext[0:1] * 64.0 + ext[2:3]).astype(jnp.int32)
            target_ref[s : s + 1, half:] = (ext[1:2] * 64.0 + ext[3:4]).astype(jnp.int32)

    row = iota((tall, cap), 0) + i * tall
    total = grad_ref[...].astype(F32)
    for s in range(slabs):
        hot = jnp.where(row == target_ref[s : s + 1], 1.0, 0.0).astype(BF16)
        total += jnp.dot(hot, arrived_ref[s, :cap], preferred_element_type=F32)
    gradh = total.astype(BF16)
    gradh_ref[...] = gradh
    pre = pre_ref[...].astype(F32)
    sig = 1.0 / (1.0 + jnp.exp(-pre))
    act = (pre * sig).astype(BF16)
    slope = sig * (1.0 + pre * (1.0 - sig))
    upd_ref[...] += lax.dot_general(act, gradh, TN, preferred_element_type=F32)
    back = lax.dot_general(gradh, w_ref[...], NT, preferred_element_type=F32)
    gp_ref[pl.ds(pl.multiple_of(i * tall, tall), tall)] = (back * slope).astype(BF16)

    @pl.when(i == pl.num_programs(0) - 1)
    def _():
        def copy(n):
            c, t = n // picks, n % picks
            at = pl.multiple_of(picks_ref[c, t] * 128, 128)
            return pltpu.make_async_copy(gp_ref.at[pl.ds(at, 128)], packed_ref.at[c, t], sem)

        lax.fori_loop(0, parts * picks, lambda n, x: (copy(n).start(), x)[1], 0)
        lax.fori_loop(0, parts * picks, lambda n, x: (copy(n).wait(), x)[1], 0)


def node_step(picks, arrived, grad, pre, w_update):
    rows, width = grad.shape
    parts, count = picks.shape
    tall = 256
    tile = pl.BlockSpec((tall, width), lambda i, *_: (i, 0))
    return pl.pallas_call(
        node_kernel,
        grid_spec=pltpu.PrefetchScalarGridSpec(
            num_scalar_prefetch=1,
            grid=(rows // tall,),
            in_specs=[
                pl.BlockSpec(arrived.shape, lambda i, *_: (0, 0, 0)),
                tile,
                tile,
                pl.BlockSpec(w_update.shape, lambda i, *_: (0, 0)),
            ],
            out_specs=[tile, pl.BlockSpec((width, width), lambda i, *_: (0, 0)), pl.BlockSpec(memory_space=pl.ANY)],
            scratch_shapes=[
                pltpu.VMEM((arrived.shape[0], arrived.shape[1] - EXT), jnp.int32),
                pltpu.VMEM((rows, width), BF16),
                pltpu.SemaphoreType.DMA,
            ],
        ),
        out_shape=[
            jax.ShapeDtypeStruct((rows, width), BF16),
            jax.ShapeDtypeStruct((width, width), F32),
            jax.ShapeDtypeStruct((parts, count, 128, width), BF16),
        ],
        compiler_params=pltpu.CompilerParams(vmem_limit_bytes=VMEM_LIMIT),
        name="node_step",
    )(picks, arrived, grad, pre, w_update)


def tile_kernel(cols_ref, got_ref, tiles_ref, gradh_ref, feats_ref, w_ref, out_ref, msg_ref, total_ref):
    r = pl.program_id(0)
    picks = got_ref.shape[1]

    @pl.when(r == 0)
    def _():
        total_ref[...] = jnp.zeros_like(total_ref)

    for t in range(picks):
        part = lax.dot_general(tiles_ref[0, t], got_ref[0, t], TN, preferred_element_type=F32)
        at = pl.ds(pl.multiple_of(cols_ref[r, t] * 128, 128), 128)
        total_ref[at] += part

    @pl.when(r == pl.num_programs(0) - 1)
    def _():
        msg = jnp.zeros(msg_ref.shape, F32)
        tall = 512
        for k in range(total_ref.shape[0] // tall):
            at = slice(k * tall, (k + 1) * tall)
            spread = total_ref[at].astype(BF16)
            msg += lax.dot_general(feats_ref[at], spread, TN, preferred_element_type=F32)
            down = lax.dot_general(spread, w_ref[...], NT, preferred_element_type=F32)
            out_ref[at] = (gradh_ref[at].astype(F32) + down).astype(BF16)
        msg_ref[...] = msg


def tile_step(cols, got, tiles, gradh, feats, w_message):
    parts, picks = cols.shape
    rows, width = gradh.shape
    whole = lambda a: pl.BlockSpec(a.shape, lambda i, *_: (0,) * a.ndim)
    return pl.pallas_call(
        tile_kernel,
        grid_spec=pltpu.PrefetchScalarGridSpec(
            num_scalar_prefetch=1,
            grid=(parts,),
            in_specs=[
                pl.BlockSpec((1, picks, 128, width), lambda i, *_: (i, 0, 0, 0)),
                pl.BlockSpec((1, picks, 128, 128), lambda i, *_: (i, 0, 0, 0)),
                whole(gradh),
                whole(feats),
                whole(w_message),
            ],
            out_specs=[whole(gradh), pl.BlockSpec((width, width), lambda i, *_: (0, 0))],
            scratch_shapes=[pltpu.VMEM((rows, width), F32)],
        ),
        out_shape=[jax.ShapeDtypeStruct((rows, width), BF16), jax.ShapeDtypeStruct((width, width), F32)],
        compiler_params=pltpu.CompilerParams(vmem_limit_bytes=VMEM_LIMIT),
        name="tile_step",
    )(cols, got, tiles, gradh, feats, w_message)


def reduce_kernel(
    parts, slabs, factor, msg_ref, upd_ref, out_msg_ref, out_upd_ref,
    mine_ref, in1, mid, in2, part_ref, all2, done, all1, s1, r1, s2, r2, s3, r3, s4, r4,
):
    b, g = lax.axis_index("blk"), lax.axis_index("grp")
    width = msg_ref.shape[0]
    rows = 2 * width // parts
    barrier = pltpu.get_barrier_semaphore()
    for k in range(1, parts):
        pl.semaphore_signal(barrier, inc=1, device_id={"blk": lax.rem(b + k, parts)}, device_id_type=MESH)
    for k in range(1, slabs):
        pl.semaphore_signal(barrier, inc=1, device_id={"grp": lax.rem(g + k, slabs)}, device_id_type=MESH)
    for k in range(parts // 2):
        mine_ref[k] = msg_ref[k * rows : (k + 1) * rows]
        mine_ref[parts // 2 + k] = upd_ref[k * rows : (k + 1) * rows]
    pl.semaphore_wait(barrier, parts + slabs - 2)

    def exchange(n, axis, me, src, dst, send, recv):
        copies = []
        for k in range(1, n):
            peer = lax.rem(me + k, n)
            copy = pltpu.make_async_remote_copy(
                src(peer), dst(k), send.at[k - 1], recv.at[k - 1], device_id={axis: peer}, device_id_type=MESH
            )
            copy.start()
            copies.append(copy)
        for copy in copies:
            copy.wait_recv()
        return copies

    sent = exchange(parts, "blk", b, lambda p: mine_ref.at[p], lambda k: in1.at[k - 1], s1, r1)
    total = mine_ref[b]
    for k in range(parts - 1):
        total += in1[k]
    for n in range(slabs):
        mid[n] = total[n // 2 * 8 : n // 2 * 8 + 8, n % 2 * 128 : n % 2 * 128 + 128]
    sent += exchange(slabs, "grp", g, lambda p: mid.at[p], lambda k: in2.at[k - 1], s2, r2)
    piece = mid[g]
    for k in range(slabs - 1):
        piece += in2[k]
    part_ref[...] = piece * factor
    all2[g] = piece * factor
    sent += exchange(slabs, "grp", g, lambda p: part_ref, lambda k: all2.at[g], s3, r3)
    for n in range(slabs):
        done[n // 2 * 8 : n // 2 * 8 + 8, n % 2 * 128 : n % 2 * 128 + 128] = all2[n]
    all1[b] = done[...]
    sent += exchange(parts, "blk", b, lambda p: done, lambda k: all1.at[b], s4, r4)
    for k in range(parts // 2):
        out_msg_ref[k * rows : (k + 1) * rows] = all1[k]
        out_upd_ref[k * rows : (k + 1) * rows] = all1[parts // 2 + k]
    for copy in sent:
        copy.wait_send()


def reduce_step(msg, upd, parts, slabs, factor):
    width = msg.shape[0]
    rows = 2 * width // parts
    vmem = pl.BlockSpec(memory_space=pltpu.VMEM)
    dma = pltpu.SemaphoreType.DMA
    return pl.pallas_call(
        functools.partial(reduce_kernel, parts, slabs, factor),
        out_shape=[jax.ShapeDtypeStruct(msg.shape, F32)] * 2,
        in_specs=[vmem] * 2,
        out_specs=[vmem] * 2,
        scratch_shapes=[
            pltpu.VMEM((parts, rows, width), F32),
            pltpu.VMEM((parts - 1, rows, width), F32),
            pltpu.VMEM((slabs, 8, 128), F32),
            pltpu.VMEM((slabs - 1, 8, 128), F32),
            pltpu.VMEM((8, 128), F32),
            pltpu.VMEM((slabs, 8, 128), F32),
            pltpu.VMEM((rows, width), F32),
            pltpu.VMEM((parts, rows, width), F32),
            dma((parts - 1,)), dma((parts - 1,)),
            dma((slabs - 1,)), dma((slabs - 1,)),
            dma((slabs - 1,)), dma((slabs - 1,)),
            dma((parts - 1,)), dma((parts - 1,)),
        ],
        compiler_params=pltpu.CompilerParams(collective_id=0, has_side_effects=True, vmem_limit_bytes=VMEM_LIMIT),
        name="reduce_step",
    )(msg, upd)


def local(
    grad_out, pre_act, node_feats, w_message, w_update, tile_vals, tile_rows, tile_cols,
    rec_slab, rec_local, rec_remote, rec_weight,
):
    grad = grad_out[0]
    rows, width = grad.shape
    slabs = lax.axis_size("grp")
    parts = lax.axis_size("blk")
    mine = lax.axis_index("blk")
    records = rec_local.shape[1]
    cap = 2 * records // slabs
    lanes = lambda a: a.reshape(records // 128, 128)
    outgoing = prep(
        lanes(rec_slab), lanes(rec_local), lanes(rec_remote), lanes(rec_weight), grad, slabs, cap
    )
    arrived = lax.all_to_all(outgoing, "grp", split_axis=0, concat_axis=0, tiled=True)
    picks = lax.dynamic_index_in_dim(tile_rows[0], mine, 1, False)
    gradh, upd, packed = node_step(picks, arrived, grad, pre_act[0], w_update)
    got = lax.all_to_all(packed, "blk", split_axis=0, concat_axis=0, tiled=True)
    feats, msg = tile_step(tile_cols[0, 0], got, tile_vals[0, 0], gradh, node_feats[0], w_message)
    factor = float((slabs * parts * rows) ** -0.5)
    msg, upd = reduce_step(msg, upd, parts, slabs, factor)
    return (feats[None], msg, upd)


def solution(mesh):
    placed = (
        P("grp", "blk", None),
        P("grp", "blk", None),
        P("grp", "blk", None),
        P(),
        P(),
        P("grp", "blk", None, None, None, None),
        P("grp", None, None, None),
        P("grp", "blk", None, None),
        P("grp", "blk", None),
        P("grp", "blk"),
        P("grp", "blk"),
        P("grp", "blk"),
    )
    return jax.shard_map(
        local,
        mesh=mesh,
        in_specs=placed,
        out_specs=(P("grp", "blk", None), P(), P()),
        check_vma=False,
    )
```

time: 687 us -> 283 us (0.41)
  waiting for transfers between devices: 377 us -> 57 us
  other arithmetic: 158 us -> 0 us
  Pallas kernels: 0 us -> 112 us
  blocking collectives: 0 us -> 101 us
  local copies, waits for them, and re-layouts: 77.3 us -> 3.95 us
  matrix products: 40.3 us -> 0 us
  between operations: 14.4 us -> 0.66 us
  starting transfers between devices: 17.5 us -> 7.76 us
    all_gather x1 -> x0, waiting for transfers between devices: 182 us -> none  [local(): piece = lax.all_gather(grad_pre, 'blk', axis=0, tiled=True)]
    psum x1 -> x0, waiting for transfers between devices: 139 us -> none  [local(): grad_message = lax.psum(msg_term, ('blk', 'grp')) * scale]
    pallas_call x0 -> x4, Pallas kernels: none -> 112 us  [the longest x1 38.1 us: reduce_step(): pl.pallas_call(functools.partial(reduce_kernel, parts, slabs, factor), ou...]
    all_to_all x0 -> x1, blocking collectives: none -> 101 us  [local(): got = lax.all_to_all(packed, 'blk', split_axis=0, concat_axis=0, tiled=True)]
    scatter-add x9 -> x0, other arithmetic: 91.1 us -> none  [the longest x1 49.2 us: local(): grad_h = grad.astype(jnp.float32).at[landing].add(arrived.reshape(-1, wid...]
    scatter x1 -> x0, other arithmetic: 48.8 us -> none  [local(): jnp.zeros((slabs * capacity, width), jnp.bfloat16).at[placed].set(payload)]
    dot_general x12 -> x0, matrix products: 40.3 us -> none  [the longest x8 23 us: local(): jnp.einsum('tij,tid->tjd', tiles_here, chosen, preferred_element_type=jnp...]
    dot_general x8 -> x0, local copies, waits for them, and re-layouts: 23.3 us -> none  [local(): jnp.einsum('tij,tid->tjd', tiles_here, chosen, preferred_element_type=jnp...]
  transfers between devices with their start and end apart: 5 -> 1, of which waited for: 4 -> 1; matrix products, arithmetic and copies ran while one was open for 10% -> 0% of each run, Pallas kernels for 0% -> 0%
where the time goes in v1:
time: 283 us
  Pallas kernels  112 us (40%)
  blocking collectives  101 us (36%)
  waiting for transfers between devices  57 us (20%)
  starting transfers between devices  7.76 us (3%)
  local copies, waits for them, and re-layouts  3.95 us (1%)
    all_to_all x1, blocking collectives, local(): got = lax.all_to_all(packed, 'blk', split_axis=0, concat_axis=0, tiled=True)  101 us
    all_to_all x1, waiting for transfers between devices, local(): lax.all_to_all(outgoing, 'grp', split_axis=0, concat_axis=0, tiled=True)  57 us
    pallas_call x1, Pallas kernels, reduce_step(): pl.pallas_call(functools.partial(reduce_kernel, parts, slabs, factor), ou...  38.1 us
    pallas_call x1, Pallas kernels, node_step(): pl.pallas_call(node_kernel, grid_spec=pltpu.PrefetchScalarGridSpec(num_sc...  32.9 us
    pallas_call x1, Pallas kernels, prep(): pl.pallas_call(prep_kernel, grid=(slabs,), out_shape=jax.ShapeDtypeStruct...  27.7 us
    pallas_call x1, Pallas kernels, tile_step(): pl.pallas_call(tile_kernel, grid_spec=pltpu.PrefetchScalarGridSpec(num_sc...  13.3 us
    all_to_all x1, starting transfers between devices, local(): lax.all_to_all(outgoing, 'grp', split_axis=0, concat_axis=0, tiled=True)  7.76 us
  transfers between devices with their start and end apart: 1, of which 1 were waited for; matrix products, arithmetic and copies ran while one was open for 0% of the time, Pallas kernels for 0%

profile of v1, /device:TPU:1, one launch (start us, length us, event | category | flops | bytes accessed | tf_op | source)
XLA Modules:
  0.0 282.7 jit_solution(14853934031975735385)
XLA Ops:
  0.6 0.0 copy-start
  0.6 27.7 %prep.1 = bf16[16,528,256]{2,1,0:T(8,128)(2,1)} custom-call(s32[32,128]{1,0:T(8,128)} %bitcast.18, s32[32,128]{1,0:T(8,128)} %bitcast.19, s32[32,128]{1,0:T(8,128)} %bitcast.20, f32[32,128]{1,0:T(8,128)} %bitcast.21, bf16[4096,256]{1,0:T(8,128)(2,1)} %bitcast.13), custom_call_target="tpu_custom_call" | custom-call | tf_op jit(solution)/shard_map/prep/pallas_call | solution.py:97
  28.4 7.8 %all-to-all-start = ((bf16[16,528,256]{2,1,0:T(8,128)(2,1)}), bf16[16,528,256]{2,1,0:T(8,128)(2,1)}, u32[]{:S(2)}, u32[]{:S(2)}) async-start(bf16[16,528,256]{2,1,0:T(8,128)(2,1)} %prep.1), calls=%async_computation | async-start | bytes 8650752 | tf_op jit(solution)/shard_map/all_to_all | solution.py:338
  36.1 0.0 copy-done
  36.1 0.6 constant_dynamic-slice_fusion
  36.7 57.0 %all-to-all-done.arrived_ref = bf16[16,528,256]{2,1,0:T(8,128)(2,1)} async-done(((bf16[16,528,256]{2,1,0:T(8,128)(2,1)}), bf16[16,528,256]{2,1,0:T(8,128)(2,1)}, u32[]{:S(2)}, u32[]{:S(2)}) %all-to-all-start) | async-done | bytes 4325408 | tf_op jit(solution)/shard_map/all_to_all | solution.py:338
  93.7 32.9 %node_step.1 = (bf16[4096,256]{1,0:T(8,128)(2,1)}, f32[256,256]{1,0:T(8,128)}, bf16[8,16,128,256]{3,2,1,0:T(8,128)(2,1)}) custom-call(s32[8,16]{1,0:T(8,128)} %bitcast.22, bf16[16,528,256]{2,1,0:T(8,128)(2,1)} %all-to-all-done.arrived_ref, bf16[4096,256]{1,0:T(8,128)(2,1)} %bitcast.14, bf16[4096,256]{1,0:T(8,128)(2,1)} %bitcast.17, bf16[256,256]{1,0:T(8,128)(2,1)} %w_ref.2), custom_call_target="tpu_custom_call" | custom-call | tf_op jit(solution)/shard_map/node_step/pallas_call | solution.py:161
  126.6 101.4 %all_to_all.10.got_ref = bf16[8,16,128,256]{3,2,1,0:T(8,128)(2,1)} all-to-all(bf16[8,16,128,256]{3,2,1,0:T(8,128)(2,1)} %get-tuple-element.10), channel_id=1, replica_groups=mesh['blk'=8,'grp'=16] {'blk'}, dimensions={0} | all-to-all | bytes 16777216 | tf_op jit(solution)/shard_map/all_to_all | solution.py:341
  228.0 13.3 %tile_step.1 = (bf16[4096,256]{1,0:T(8,128)(2,1)}, f32[256,256]{1,0:T(8,128)}) custom-call(s32[8,16]{1,0:T(8,128)} %bitcast.23, bf16[8,16,128,256]{3,2,1,0:T(8,128)(2,1)} %all_to_all.10.got_ref, bf16[8,16,128,128]{3,2,1,0:T(8,128)(2,1)} %bitcast.15, bf16[4096,256]{1,0:T(8,128)(2,1)} %get-tuple-element.11.gradh_ref, bf16[4096,256]{1,0:T(8,128)(2,1)} %bitcast.16, ...), custom_call_target="tpu_custom_call" | custom-call | tf_op jit(solution)/shard_map/tile_step/pallas_call | solution.py:219
  241.3 38.1 %reduce_step.1 = (f32[256,256]{1,0:T(8,128)}, f32[256,256]{1,0:T(8,128)}) custom-call(f32[256,256]{1,0:T(8,128)} %get-tuple-element.13.msg_ref, f32[256,256]{1,0:T(8,128)} %get-tuple-element.14.upd_ref), custom_call_target="tpu_custom_call" | custom-call | tf_op jit(solution)/shard_map/reduce_step/pallas_call | solution.py:299
  279.4 1.7 copy.19
  281.1 1.7 copy.20
Async XLA Ops:
  0.6 35.5 %copy-start = (s32[1,8,8,16]{3,2,1,0:T(8,128)S(1)}, s32[1,8,8,16]{3,2,1,0:T(8,128)}, u32[]{:S(2)}) copy-start(s32[1,8,8,16]{3,2,1,0:T(8,128)} %param.18) | copy-start | bytes 12292
  28.4 65.4 %all-to-all-start = ((bf16[16,528,256]{2,1,0:T(8,128)(2,1)}), bf16[16,528,256]{2,1,0:T(8,128)(2,1)}, u32[]{:S(2)}, u32[]{:S(2)}) async-start(bf16[16,528,256]{2,1,0:T(8,128)(2,1)} %prep.1), calls=%async_computation | async-start | bytes 8650752 | tf_op jit(solution)/shard_map/all_to_all | solution.py:338

commit v2 on v1

v2 whole, which is shorter than its diff:
```python
import functools

import jax
import jax.numpy as jnp
from jax import lax
from jax.experimental import pallas as pl
from jax.experimental.pallas import tpu as pltpu
from jax.sharding import PartitionSpec as P

F32 = jnp.float32
BF16 = jnp.bfloat16
MESH = pl.DeviceIdType.MESH
NT = (((1,), (1,)), ((), ()))
TN = (((0,), (0,)), ((), ()))
EXT = 16
VMEM_LIMIT = 56 * 1024 * 1024


def iota(shape, dim):
    return lax.broadcasted_iota(jnp.int32, shape, dim)


def index_tables(slab_ref, local_ref, remote_ref, weight_ref, node_ref, scale_ref, ext_ref):
    slabs, cap = node_ref.shape[0], node_ref.shape[1]
    chunks = slab_ref.shape[0]
    slab = slab_ref[...]
    ids = iota((chunks, slabs, 128), 1)
    choose = jnp.where(ids == slab[:, None, :], 1.0, 0.0)
    flat = choose.reshape(chunks * slabs, 128)
    flat16 = flat.astype(BF16)
    upper = jnp.where(iota((128, 128), 0) < iota((128, 128), 1), 1.0, 0.0).astype(BF16)
    prefix = jnp.dot(flat16, upper, preferred_element_type=F32)
    totals = jnp.dot(flat16, jnp.ones((128, 128), BF16), preferred_element_type=F32)
    size = chunks * slabs
    row, col = iota((size, size), 0), iota((size, size), 1)
    earlier = (col < row) & (lax.rem(col, slabs) == lax.rem(row, slabs))
    offset = jnp.dot(jnp.where(earlier, 1.0, 0.0).astype(BF16), totals.astype(BF16), preferred_element_type=F32)
    place = ((prefix + offset) * flat).reshape(chunks, slabs, 128).sum(axis=1).astype(jnp.int32)
    remote, local, weight = remote_ref[...], local_ref[...], weight_ref[...]
    first = weight.astype(BF16).astype(F32)
    second = (weight - first).astype(BF16).astype(F32)
    third = weight - first - second
    values = [
        (remote // 64).astype(F32),
        (remote % 64).astype(F32),
        (local // 64).astype(F32),
        (local % 64).astype(F32),
        first,
        second,
        third,
        jnp.ones_like(weight),
    ]
    table = jnp.zeros((len(values) * slabs, cap), F32)
    for c in range(chunks):
        left = jnp.concatenate([choose[c] * v[c : c + 1] for v in values], axis=0).astype(BF16)
        right = jnp.where(iota((cap, 128), 0) == place[c : c + 1], 1.0, 0.0).astype(BF16)
        table += lax.dot_general(left, right, NT, preferred_element_type=F32)
    valid = table[7 * slabs : 8 * slabs]
    upper_part = jnp.where(valid > 0.5, table[:slabs], 64.0)
    lower_part = table[slabs : 2 * slabs]
    half = cap // 2
    for s in range(slabs):
        rows = [part[s : s + 1, q * half : (q + 1) * half] for part in (upper_part, lower_part) for q in range(2)]
        block = jnp.concatenate(rows + [jnp.zeros((EXT - 4, half), F32)], axis=0)
        ext_ref[s] = block.astype(BF16)
    turned = jnp.transpose(table)
    for s in range(slabs):
        at = lambda v: turned[:, v * slabs + s : v * slabs + s + 1]
        node_ref[s] = jnp.broadcast_to((at(2) * 64.0 + at(3)).astype(jnp.int32), (cap, 128))
        scale_ref[s] = jnp.broadcast_to(at(4) + at(5) + at(6), (cap, 128))


FAR = ((2, 1), (1, 1), (3, 1), (0, 1), (2, 0), (1, 0), (3, 0))


def main_kernel(
    parts, slabs,
    picks_ref, slab_ref, local_ref, remote_ref, weight_ref, w_ref, grad_hbm, pre_hbm,
    gradh_hbm, upd_ref, got_hbm,
    node_ref, scale_ref, ext_ref, out_buf, in_buf, grad_ref, pre_ref, gradh_ref, acc_ref, gp_ref, stage_ref,
    load_sem, rec_send, rec_recv, blk_send, blk_recv, store_sem,
):
    b, g = lax.axis_index("blk"), lax.axis_index("grp")
    y, xh = b // 2, b % 2
    xl, z, core = g // 8, (g // 2) % 4, g % 2
    cap = node_ref.shape[1]
    half = cap // 2
    nodes, width = acc_ref.shape
    picks = stage_ref.shape[1]

    load_grad = pltpu.make_async_copy(grad_hbm, grad_ref, load_sem.at[0])
    load_pre = pltpu.make_async_copy(pre_hbm, pre_ref, load_sem.at[1])
    load_grad.start()
    load_pre.start()

    def rec_peer(n):
        q = n // 4
        dz, dx, dc = (n % 4 + 1) % 4, 1 - n // 8, (q + q // 2) % 2
        return ((xl + dx) % 2 * 4 + (z + dz) % 4) * 2 + (core + dc) % 2

    def blk_peer(n):
        dy, dx = FAR[n]
        return (y + dy) % 4 * 2 + (xh + dx) % 2

    barrier = pltpu.get_barrier_semaphore()
    for n in range(slabs - 1):
        pl.semaphore_signal(barrier, inc=1, device_id={"grp": rec_peer(n)}, device_id_type=MESH)
    for n in range(parts - 1):
        pl.semaphore_signal(barrier, inc=1, device_id={"blk": blk_peer(n)}, device_id_type=MESH)

    index_tables(slab_ref, local_ref, remote_ref, weight_ref, node_ref, scale_ref, ext_ref)
    load_grad.wait()
    pl.semaphore_wait(barrier, slabs + parts - 2)

    def rec_copy(n):
        return pltpu.make_async_remote_copy(
            out_buf.at[n], in_buf.at[n], rec_send.at[n], rec_recv.at[n],
            device_id={"grp": rec_peer(n)}, device_id_type=MESH,
        )

    own = slabs - 1
    own_copy = pltpu.make_async_copy(out_buf.at[own], in_buf.at[own], rec_recv.at[own])
    wide = 1024

    def gather(n, _):
        s = rec_peer(n)
        node = node_ref[s]
        total = jnp.zeros((cap, width), F32)
        for k in range(nodes // wide):
            pieces = [
                jnp.where(node == iota((1, 128), 1) + (k * wide + j * 128), 1.0, 0.0).astype(BF16)
                for j in range(wide // 128)
            ]
            total += jnp.dot(
                jnp.concatenate(pieces, axis=1), grad_ref[k * wide : (k + 1) * wide], preferred_element_type=F32
            )
        scale = scale_ref[s]
        out_buf[n, :cap] = (total * jnp.concatenate([scale, scale], axis=1)).astype(BF16)
        out_buf[n, cap:] = ext_ref[s]

        @pl.when(n < own)
        def _():
            rec_copy(n).start()

        return 0

    lax.fori_loop(0, slabs, gather, 0)
    own_copy.start()
    acc_ref[...] = grad_ref[...].astype(F32)
    own_copy.wait()

    tall = 512

    def scatter(m, _):
        n = (m + own) % slabs

        @pl.when(m > 0)
        def _():
            rec_copy(n).wait_recv()

        ext = in_buf[n, cap:].astype(F32)
        targets = [(ext[q : q + 1] * 64.0 + ext[2 + q : 3 + q]).astype(jnp.int32) for q in range(2)]
        block = in_buf[n, :cap]

        def rows(i, _):
            at = pl.ds(pl.multiple_of(i * tall, tall), tall)
            row = iota((tall, 128), 0)
            pieces = [
                jnp.where(row == targets[j // 2][:, j % 2 * 128 : j % 2 * 128 + 128] - i * tall, 1.0, 0.0).astype(BF16)
                for j in range(cap // 128)
            ]
            acc_ref[at] += jnp.dot(jnp.concatenate(pieces, axis=1), block, preferred_element_type=F32)
            return 0

        lax.fori_loop(0, nodes // tall, rows, 0)
        return 0

    lax.fori_loop(0, slabs, scatter, 0)

    load_pre.wait()
    upd_ref[...] = jnp.zeros_like(upd_ref)

    def finish(i, _):
        at = pl.ds(pl.multiple_of(i * 256, 256), 256)
        gradh = acc_ref[at].astype(BF16)
        gradh_ref[at] = gradh
        pre = pre_ref[at].astype(F32)
        sig = 1.0 / (1.0 + jnp.exp(-pre))
        act = (pre * sig).astype(BF16)
        slope = sig * (1.0 + pre * (1.0 - sig))
        back = lax.dot_general(gradh, w_ref[...], NT, preferred_element_type=F32)
        gp_ref[pl.ds(i * 2, 2)] = (back * slope).astype(BF16).reshape(2, 128, width)
        upd_ref[...] += lax.dot_general(act, gradh, TN, preferred_element_type=F32)
        return 0

    lax.fori_loop(0, nodes // 256, finish, 0)
    store_gradh = pltpu.make_async_copy(gradh_ref, gradh_hbm, store_sem.at[0])
    store_gradh.start()

    def pack(n, c):
        def one(t, _):
            stage_ref[n, t] = gp_ref[picks_ref[c, b, t]]
            return 0

        lax.fori_loop(0, picks, one, 0)

    sends = []
    for n in range(parts - 1):
        pack(n, blk_peer(n))
        copy = pltpu.make_async_remote_copy(
            stage_ref.at[n], got_hbm.at[b], blk_send.at[n], blk_recv.at[n],
            device_id={"blk": blk_peer(n)}, device_id_type=MESH,
        )
        copy.start()
        sends.append(copy)
    pack(parts - 1, b)
    keep = pltpu.make_async_copy(stage_ref.at[parts - 1], got_hbm.at[b], store_sem.at[1])
    keep.start()
    lax.fori_loop(0, slabs - 1, lambda n, x: (rec_copy(n).wait_send(), x)[1], 0)
    for copy in sends:
        copy.wait()
    keep.wait()
    store_gradh.wait()


def main_step(picks, slab, local, remote, weight, w_update, grad, pre, slabs, parts, cap):
    nodes, width = grad.shape
    count = picks.shape[-1]
    vmem = pl.BlockSpec(memory_space=pltpu.VMEM)
    hbm = pl.BlockSpec(memory_space=pl.ANY)
    dma = pltpu.SemaphoreType.DMA
    return pl.pallas_call(
        functools.partial(main_kernel, parts, slabs),
        out_shape=[
            jax.ShapeDtypeStruct((nodes, width), BF16),
            jax.ShapeDtypeStruct((width, width), F32),
            jax.ShapeDtypeStruct((parts, count, 128, width), BF16),
        ],
        in_specs=[pl.BlockSpec(memory_space=pltpu.SMEM)] + [vmem] * 5 + [hbm] * 2,
        out_specs=[hbm, vmem, hbm],
        scratch_shapes=[
            pltpu.VMEM((slabs, cap, 128), jnp.int32),
            pltpu.VMEM((slabs, cap, 128), F32),
            pltpu.VMEM((slabs, EXT, width), BF16),
            pltpu.VMEM((slabs, cap + EXT, width), BF16),
            pltpu.VMEM((slabs, cap + EXT, width), BF16),
            pltpu.VMEM((nodes, width), BF16),
            pltpu.VMEM((nodes, width), BF16),
            pltpu.VMEM((nodes, width), BF16),
            pltpu.VMEM((nodes, width), F32),
            pltpu.VMEM((nodes // 128, 128, width), BF16),
            pltpu.VMEM((parts, count, 128, width), BF16),
            dma((2,)), dma((slabs - 1,)), dma((slabs,)), dma((parts - 1,)), dma((parts - 1,)), dma((2,)),
        ],
        compiler_params=pltpu.CompilerParams(collective_id=1, has_side_effects=True, vmem_limit_bytes=VMEM_LIMIT),
        name="main_step",
    )(picks, slab, local, remote, weight, w_update, grad, pre)


def tile_kernel(cols_ref, got_ref, tiles_ref, gradh_ref, feats_ref, w_ref, out_ref, msg_ref, total_ref):
    r = pl.program_id(0)
    picks = got_ref.shape[1]

    @pl.when(r == 0)
    def _():
        total_ref[...] = jnp.zeros_like(total_ref)

    for t in range(picks):
        part = lax.dot_general(tiles_ref[0, t], got_ref[0, t], TN, preferred_element_type=F32)
        at = pl.ds(pl.multiple_of(cols_ref[r, t] * 128, 128), 128)
        total_ref[at] += part

    @pl.when(r == pl.num_programs(0) - 1)
    def _():
        msg = jnp.zeros(msg_ref.shape, F32)
        tall = 512
        for k in range(total_ref.shape[0] // tall):
            at = slice(k * tall, (k + 1) * tall)
            spread = total_ref[at].astype(BF16)
            msg += lax.dot_general(feats_ref[at], spread, TN, preferred_element_type=F32)
            down = lax.dot_general(spread, w_ref[...], NT, preferred_element_type=F32)
            out_ref[at] = (gradh_ref[at].astype(F32) + down).astype(BF16)
        msg_ref[...] = msg


def tile_step(cols, got, tiles, gradh, feats, w_message):
    parts, picks = cols.shape
    rows, width = gradh.shape
    whole = lambda a: pl.BlockSpec(a.shape, lambda i, *_: (0,) * a.ndim)
    return pl.pallas_call(
        tile_kernel,
        grid_spec=pltpu.PrefetchScalarGridSpec(
            num_scalar_prefetch=1,
            grid=(parts,),
            in_specs=[
                pl.BlockSpec((1, picks, 128, width), lambda i, *_: (i, 0, 0, 0)),
                pl.BlockSpec((1, picks, 128, 128), lambda i, *_: (i, 0, 0, 0)),
                whole(gradh),
                whole(feats),
                whole(w_message),
            ],
            out_specs=[whole(gradh), pl.BlockSpec((width, width), lambda i, *_: (0, 0))],
            scratch_shapes=[pltpu.VMEM((rows, width), F32)],
        ),
        out_shape=[jax.ShapeDtypeStruct((rows, width), BF16), jax.ShapeDtypeStruct((width, width), F32)],
        compiler_params=pltpu.CompilerParams(vmem_limit_bytes=VMEM_LIMIT),
        name="tile_step",
    )(cols, got, tiles, gradh, feats, w_message)


def reduce_kernel(
    parts, slabs, factor, msg_ref, upd_ref, out_msg_ref, out_upd_ref,
    mine_ref, in1, mid, in2, part_ref, all2, done, all1, s1, r1, s2, r2, s3, r3, s4, r4,
):
    b, g = lax.axis_index("blk"), lax.axis_index("grp")
    width = msg_ref.shape[0]
    rows = 2 * width // parts
    barrier = pltpu.get_barrier_semaphore()
    for k in range(1, parts):
        pl.semaphore_signal(barrier, inc=1, device_id={"blk": lax.rem(b + k, parts)}, device_id_type=MESH)
    for k in range(1, slabs):
        pl.semaphore_signal(barrier, inc=1, device_id={"grp": lax.rem(g + k, slabs)}, device_id_type=MESH)
    for k in range(parts // 2):
        mine_ref[k] = msg_ref[k * rows : (k + 1) * rows]
        mine_ref[parts // 2 + k] = upd_ref[k * rows : (k + 1) * rows]
    pl.semaphore_wait(barrier, parts + slabs - 2)

    def exchange(n, axis, me, src, dst, send, recv):
        copies = []
        for k in range(1, n):
            peer = lax.rem(me + k, n)
            copy = pltpu.make_async_remote_copy(
                src(peer), dst(k), send.at[k - 1], recv.at[k - 1], device_id={axis: peer}, device_id_type=MESH
            )
            copy.start()
            copies.append(copy)
        for copy in copies:
            copy.wait_recv()
        return copies

    sent = exchange(parts, "blk", b, lambda p: mine_ref.at[p], lambda k: in1.at[k - 1], s1, r1)
    total = mine_ref[b]
    for k in range(parts - 1):
        total += in1[k]
    for n in range(slabs):
        mid[n] = total[n // 2 * 8 : n // 2 * 8 + 8, n % 2 * 128 : n % 2 * 128 + 128]
    sent += exchange(slabs, "grp", g, lambda p: mid.at[p], lambda k: in2.at[k - 1], s2, r2)
    piece = mid[g]
    for k in range(slabs - 1):
        piece += in2[k]
    part_ref[...] = piece * factor
    all2[g] = piece * factor
    sent += exchange(slabs, "grp", g, lambda p: part_ref, lambda k: all2.at[g], s3, r3)
    for n in range(slabs):
        done[n // 2 * 8 : n // 2 * 8 + 8, n % 2 * 128 : n % 2 * 128 + 128] = all2[n]
    all1[b] = done[...]
    sent += exchange(parts, "blk", b, lambda p: done, lambda k: all1.at[b], s4, r4)
    for k in range(parts // 2):
        out_msg_ref[k * rows : (k + 1) * rows] = all1[k]
        out_upd_ref[k * rows : (k + 1) * rows] = all1[parts // 2 + k]
    for copy in sent:
        copy.wait_send()


def reduce_step(msg, upd, parts, slabs, factor):
    width = msg.shape[0]
    rows = 2 * width // parts
    vmem = pl.BlockSpec(memory_space=pltpu.VMEM)
    dma = pltpu.SemaphoreType.DMA
    return pl.pallas_call(
        functools.partial(reduce_kernel, parts, slabs, factor),
        out_shape=[jax.ShapeDtypeStruct(msg.shape, F32)] * 2,
        in_specs=[vmem] * 2,
        out_specs=[vmem] * 2,
        scratch_shapes=[
            pltpu.VMEM((parts, rows, width), F32),
            pltpu.VMEM((parts - 1, rows, width), F32),
            pltpu.VMEM((slabs, 8, 128), F32),
            pltpu.VMEM((slabs - 1, 8, 128), F32),
            pltpu.VMEM((8, 128), F32),
            pltpu.VMEM((slabs, 8, 128), F32),
            pltpu.VMEM((rows, width), F32),
            pltpu.VMEM((parts, rows, width), F32),
            dma((parts - 1,)), dma((parts - 1,)),
            dma((slabs - 1,)), dma((slabs - 1,)),
            dma((slabs - 1,)), dma((slabs - 1,)),
            dma((parts - 1,)), dma((parts - 1,)),
        ],
        compiler_params=pltpu.CompilerParams(collective_id=0, has_side_effects=True, vmem_limit_bytes=VMEM_LIMIT),
        name="reduce_step",
    )(msg, upd)


def local(
    grad_out, pre_act, node_feats, w_message, w_update, tile_vals, tile_rows, tile_cols,
    rec_slab, rec_local, rec_remote, rec_weight,
):
    grad = grad_out[0]
    rows, width = grad.shape
    slabs = lax.axis_size("grp")
    parts = lax.axis_size("blk")
    records = rec_local.shape[1]
    cap = 2 * records // slabs
    lanes = lambda a: a.reshape(records // 128, 128)
    gradh, upd, got = main_step(
        tile_rows[0], lanes(rec_slab), lanes(rec_local), lanes(rec_remote), lanes(rec_weight),
        w_update, grad, pre_act[0], slabs, parts, cap,
    )
    feats, msg = tile_step(tile_cols[0, 0], got, tile_vals[0, 0], gradh, node_feats[0], w_message)
    factor = float((slabs * parts * rows) ** -0.5)
    msg, upd = reduce_step(msg, upd, parts, slabs, factor)
    return (feats[None], msg, upd)


def solution(mesh):
    placed = (
        P("grp", "blk", None),
        P("grp", "blk", None),
        P("grp", "blk", None),
        P(),
        P(),
        P("grp", "blk", None, None, None, None),
        P("grp", None, None, None),
        P("grp", "blk", None, None),
        P("grp", "blk", None),
        P("grp", "blk"),
        P("grp", "blk"),
        P("grp", "blk"),
    )
    return jax.shard_map(
        local,
        mesh=mesh,
        in_specs=placed,
        out_specs=(P("grp", "blk", None), P(), P()),
        check_vma=False,
    )
```

time: 283 us -> 228 us (0.81)
  Pallas kernels: 112 us -> 224 us
  blocking collectives: 101 us -> 0 us
  waiting for transfers between devices: 57 us -> 0 us
  starting transfers between devices: 7.76 us -> 0 us
    pallas_call x2 -> x1, Pallas kernels: 60.6 us -> 180 us  [main_step(): pl.pallas_call(functools.partial(main_kernel, parts, slabs), out_shape=[j...]
    all_to_all x1 -> x0, blocking collectives: 101 us -> none  [local(): got = lax.all_to_all(packed, 'blk', split_axis=0, concat_axis=0, tiled=True)]
    all_to_all x1 -> x0, waiting for transfers between devices: 57 us -> none  [local(): lax.all_to_all(outgoing, 'grp', split_axis=0, concat_axis=0, tiled=True)]
    all_to_all x1 -> x0, starting transfers between devices: 7.76 us -> none  [local(): lax.all_to_all(outgoing, 'grp', split_axis=0, concat_axis=0, tiled=True)]
    pallas_call x1, Pallas kernels: 38.1 us -> 31.2 us  [reduce_step(): pl.pallas_call(functools.partial(reduce_kernel, parts, slabs, factor), ou...]
  transfers between devices with their start and end apart: 1 -> 0, of which waited for: 1 -> 0; matrix products, arithmetic and copies ran while one was open for 0% -> 0% of each run, Pallas kernels for 0% -> 0%
where the time goes in v2:
time: 228 us
  Pallas kernels  224 us (98%)
  local copies, waits for them, and re-layouts  3.34 us (1%)
    pallas_call x1, Pallas kernels, main_step(): pl.pallas_call(functools.partial(main_kernel, parts, slabs), out_shape=[j...  180 us
    pallas_call x1, Pallas kernels, reduce_step(): pl.pallas_call(functools.partial(reduce_kernel, parts, slabs, factor), ou...  31.2 us
    pallas_call x1, Pallas kernels, tile_step(): pl.pallas_call(tile_kernel, grid_spec=pltpu.PrefetchScalarGridSpec(num_sc...  13.3 us

profile of v2, /device:TPU:1, one launch (start us, length us, event | category | flops | bytes accessed | tf_op | source)
XLA Modules:
  0.0 228.1 jit_solution(15263977015794180647)
XLA Ops:
  0.6 179.6 %main_step.1 = (bf16[4096,256]{1,0:T(8,128)(2,1)}, f32[256,256]{1,0:T(8,128)}, bf16[8,16,128,256]{3,2,1,0:T(8,128)(2,1)}) custom-call(s32[8,8,16]{2,1,0:T(8,128)} %bitcast.15, s32[32,128]{1,0:T(8,128)} %bitcast.16, s32[32,128]{1,0:T(8,128)} %bitcast.17, s32[32,128]{1,0:T(8,128)} %bitcast.18, f32[32,128]{1,0:T(8,128)} %bitcast.19, bf16[256,256]{1,0:T(8,128)(2,1)} %w_ref.2, ...), custom_call_target="tpu_custom_call" | custom-call | tf_op jit(solution)/shard_map/main_step/pallas_call | solution.py:232
  180.2 13.3 %tile_step.1 = (bf16[4096,256]{1,0:T(8,128)(2,1)}, f32[256,256]{1,0:T(8,128)}) custom-call(s32[8,16]{1,0:T(8,128)} %bitcast.20, bf16[8,16,128,256]{3,2,1,0:T(8,128)(2,1)} %get-tuple-element.10.got_ref, bf16[8,16,128,128]{3,2,1,0:T(8,128)(2,1)} %bitcast.11, bf16[4096,256]{1,0:T(8,128)(2,1)} %get-tuple-element.11.gradh_ref, bf16[4096,256]{1,0:T(8,128)(2,1)} %bitcast.12, ...), custom_call_target="tpu_custom_call" | custom-call | tf_op jit(solution)/shard_map/tile_step/pallas_call | solution.py:290
  193.5 31.2 %reduce_step.1 = (f32[256,256]{1,0:T(8,128)}, f32[256,256]{1,0:T(8,128)}) custom-call(f32[256,256]{1,0:T(8,128)} %get-tuple-element.13.msg_ref, f32[256,256]{1,0:T(8,128)} %get-tuple-element.14.upd_ref), custom_call_target="tpu_custom_call" | custom-call | tf_op jit(solution)/shard_map/reduce_step/pallas_call | solution.py:370
  224.8 1.7 copy.17
  226.4 1.7 copy.18

commit v3 on v2

--- a/solution.py
+++ b/solution.py
@@ -41,8 +41,8 @@
     second = (weight - first).astype(BF16).astype(F32)
     third = weight - first - second
     values = [
-        (remote // 64).astype(F32),
-        (remote % 64).astype(F32),
+        (remote // 256).astype(F32),
+        (remote % 256).astype(F32),
         (local // 64).astype(F32),
         (local % 64).astype(F32),
         first,
@@ -70,15 +70,116 @@
         scale_ref[s] = jnp.broadcast_to(at(4) + at(5) + at(6), (cap, 128))
 
 
+def sum_scratch(parts, slabs, width):
+    rows = width // parts
+    dma = pltpu.SemaphoreType.DMA
+    return [
+        pltpu.VMEM((parts, rows, width), F32),
+        pltpu.VMEM((parts - 1, rows, width), F32),
+        pltpu.VMEM((slabs, 8, 128), F32),
+        pltpu.VMEM((slabs - 1, 8, 128), F32),
+        pltpu.VMEM((8, 128), F32),
+        pltpu.VMEM((slabs, 8, 128), F32),
+        pltpu.VMEM((rows, width), F32),
+        pltpu.VMEM((parts, rows, width), F32),
+        dma((parts - 1,)), dma((parts - 1,)),
+        dma((slabs - 1,)), dma((slabs - 1,)),
+        dma((slabs - 1,)), dma((slabs - 1,)),
+        dma((parts - 1,)), dma((parts - 1,)),
+    ]
+
+
+def sum_stages(parts, slabs, factor, term_ref, out_ref, scratch):
+    mine, in1, mid, in2, part, all2, done, all1, s1, r1, s2, r2, s3, r3, s4, r4 = scratch
+    b, g = lax.axis_index("blk"), lax.axis_index("grp")
+    width = term_ref.shape[0]
+    rows = width // parts
+    sent = []
+
+    def exchange(n, axis, me, src, dst, send, recv):
+        copies = []
+        for k in range(1, n):
+            peer = lax.rem(me + k, n)
+            copy = pltpu.make_async_remote_copy(
+                src(peer), dst(k), send.at[k - 1], recv.at[k - 1], device_id={axis: peer}, device_id_type=MESH
+            )
+            copy.start()
+            copies.append(copy)
+        sent.extend(copies)
+        return copies
+
+    def begin():
+        for k in range(parts):
+            mine[k] = term_ref[k * rows : (k + 1) * rows]
+        mid[...] = jnp.zeros_like(mid)
+        return exchange(parts, "blk", b, lambda p: mine.at[p], lambda k: in1.at[k - 1], s1, r1)
+
+    def end(copies):
+        for copy in copies:
+            copy.wait_recv()
+        total = mine[b]
+        for k in range(parts - 1):
+            total += in1[k]
+        high = rows * 2 // slabs
+        spots = [(slice(n // 2 * high, (n // 2 + 1) * high), slice(n % 2 * 128, n % 2 * 128 + 128)) for n in range(slabs)]
+        for n in range(slabs):
+            mid[n, :high] = total[spots[n]]
+        for copy in exchange(slabs, "grp", g, lambda p: mid.at[p], lambda k: in2.at[k - 1], s2, r2):
+            copy.wait_recv()
+        piece = mid[g]
+        for k in range(slabs - 1):
+            piece += in2[k]
+        part[...] = piece * factor
+        all2[g] = piece * factor
+        for copy in exchange(slabs, "grp", g, lambda p: part, lambda k: all2.at[g], s3, r3):
+            copy.wait_recv()
+        for n in range(slabs):
+            done[spots[n]] = all2[n, :high]
+        all1[b] = done[...]
+        for copy in exchange(parts, "blk", b, lambda p: done, lambda k: all1.at[b], s4, r4):
+            copy.wait_recv()
+        for k in range(parts):
+            out_ref[k * rows : (k + 1) * rows] = all1[k]
+        for copy in sent:
+            copy.wait_send()
+
+    return begin, end
+
+
+def reduce_kernel(parts, slabs, factor, term_ref, out_ref, *scratch):
+    b, g = lax.axis_index("blk"), lax.axis_index("grp")
+    barrier = pltpu.get_barrier_semaphore()
+    for k in range(1, parts):
+        pl.semaphore_signal(barrier, inc=1, device_id={"blk": lax.rem(b + k, parts)}, device_id_type=MESH)
+    for k in range(1, slabs):
+        pl.semaphore_signal(barrier, inc=1, device_id={"grp": lax.rem(g + k, slabs)}, device_id_type=MESH)
+    begin, end = sum_stages(parts, slabs, factor, term_ref, out_ref, scratch)
+    pl.semaphore_wait(barrier, parts + slabs - 2)
+    end(begin())
+
+
+def reduce_step(term, parts, slabs, factor):
+    vmem = pl.BlockSpec(memory_space=pltpu.VMEM)
+    return pl.pallas_call(
+        functools.partial(reduce_kernel, parts, slabs, factor),
+        out_shape=jax.ShapeDtypeStruct(term.shape, F32),
+        in_specs=[vmem],
+        out_specs=vmem,
+        scratch_shapes=sum_scratch(parts, slabs, term.shape[0]),
+        compiler_params=pltpu.CompilerParams(collective_id=0, has_side_effects=True, vmem_limit_bytes=VMEM_LIMIT),
+        name="reduce_step",
+    )(term)
+
+
 FAR = ((2, 1), (1, 1), (3, 1), (0, 1), (2, 0), (1, 0), (3, 0))
 
 
 def main_kernel(
-    parts, slabs,
+    parts, slabs, factor,
     picks_ref, slab_ref, local_ref, remote_ref, weight_ref, w_ref, grad_hbm, pre_hbm,
     gradh_hbm, upd_ref, got_hbm,
     node_ref, scale_ref, ext_ref, out_buf, in_buf, grad_ref, pre_ref, gradh_ref, acc_ref, gp_ref, stage_ref,
-    load_sem, rec_send, rec_recv, blk_send, blk_recv, store_sem,
+    load_sem, rec_send, rec_recv, blk_send, blk_recv, store_sem, term_ref, *scratch,
 ):
     b, g = lax.axis_index("blk"), lax.axis_index("grp")
     y, xh = b // 2, b % 2
@@ -149,7 +250,7 @@
     acc_ref[...] = grad_ref[...].astype(F32)
     own_copy.wait()
 
-    tall = 512
+    tall = 1024
 
     def scatter(m, _):
         n = (m + own) % slabs
@@ -159,26 +260,23 @@
             rec_copy(n).wait_recv()
 
         ext = in_buf[n, cap:].astype(F32)
-        targets = [(ext[q : q + 1] * 64.0 + ext[2 + q : 3 + q]).astype(jnp.int32) for q in range(2)]
+        lane = lambda q: jnp.concatenate([ext[q : q + 1], ext[q + 1 : q + 2]], axis=1).astype(jnp.int32)
+        high, low = lane(0), lane(2)
+        base = jnp.where(iota((256, cap), 0) == low, 1.0, 0.0).astype(BF16).reshape(16, 16, cap)
         block = in_buf[n, :cap]
-
-        def rows(i, _):
-            at = pl.ds(pl.multiple_of(i * tall, tall), tall)
-            row = iota((tall, 128), 0)
-            pieces = [
-                jnp.where(row == targets[j // 2][:, j % 2 * 128 : j % 2 * 128 + 128] - i * tall, 1.0, 0.0).astype(BF16)
-                for j in range(cap // 128)
-            ]
-            acc_ref[at] += jnp.dot(jnp.concatenate(pieces, axis=1), block, preferred_element_type=F32)
-            return 0
-
-        lax.fori_loop(0, nodes // tall, rows, 0)
+        for i in range(nodes // tall):
+            pieces = []
+            for c in range(i * tall // 256, (i + 1) * tall // 256):
+                mask = jnp.where(jnp.broadcast_to(high, (16, cap)) == c, 1.0, 0.0).astype(BF16)
+                pieces.append((base * mask[None]).reshape(256, cap))
+            at = slice(i * tall, (i + 1) * tall)
+            acc_ref[at] += jnp.dot(jnp.concatenate(pieces, axis=0), block, preferred_element_type=F32)
         return 0
 
     lax.fori_loop(0, slabs, scatter, 0)
 
     load_pre.wait()
-    upd_ref[...] = jnp.zeros_like(upd_ref)
+    term_ref[...] = jnp.zeros_like(term_ref)
 
     def finish(i, _):
         at = pl.ds(pl.multiple_of(i * 256, 256), 256)
@@ -190,12 +288,14 @@
         slope = sig * (1.0 + pre * (1.0 - sig))
         back = lax.dot_general(gradh, w_ref[...], NT, preferred_element_type=F32)
         gp_ref[pl.ds(i * 2, 2)] = (back * slope).astype(BF16).reshape(2, 128, width)
-        upd_ref[...] += lax.dot_general(act, gradh, TN, preferred_element_type=F32)
+        term_ref[...] += lax.dot_general(act, gradh, TN, preferred_element_type=F32)
         return 0
 
     lax.fori_loop(0, nodes // 256, finish, 0)
     store_gradh = pltpu.make_async_copy(gradh_ref, gradh_hbm, store_sem.at[0])
     store_gradh.start()
+    begin, end = sum_stages(parts, slabs, factor, term_ref, upd_ref, scratch)
+    first = begin()
 
     def pack(n, c):
         def one(t, _):
@@ -216,6 +316,7 @@
     pack(parts - 1, b)
     keep = pltpu.make_async_copy(stage_ref.at[parts - 1], got_hbm.at[b], store_sem.at[1])
     keep.start()
+    end(first)
     lax.fori_loop(0, slabs - 1, lambda n, x: (rec_copy(n).wait_send(), x)[1], 0)
     for copy in sends:
         copy.wait()
@@ -223,14 +324,14 @@
     store_gradh.wait()
 
 
-def main_step(picks, slab, local, remote, weight, w_update, grad, pre, slabs, parts, cap):
+def main_step(picks, slab, local, remote, weight, w_update, grad, pre, slabs, parts, cap, factor):
     nodes, width = grad.shape
     count = picks.shape[-1]
     vmem = pl.BlockSpec(memory_space=pltpu.VMEM)
     hbm = pl.BlockSpec(memory_space=pl.ANY)
     dma = pltpu.SemaphoreType.DMA
     return pl.pallas_call(
-        functools.partial(main_kernel, parts, slabs),
+        functools.partial(main_kernel, parts, slabs, factor),
         out_shape=[
             jax.ShapeDtypeStruct((nodes, width), BF16),
             jax.ShapeDtypeStruct((width, width), F32),
@@ -251,7 +352,9 @@
             pltpu.VMEM((nodes // 128, 128, width), BF16),
             pltpu.VMEM((parts, count, 128, width), BF16),
             dma((2,)), dma((slabs - 1,)), dma((slabs,)), dma((parts - 1,)), dma((parts - 1,)), dma((2,)),
-        ],
+            pltpu.VMEM((width, width), F32),
+        ]
+        + sum_scratch(parts, slabs, width),
         compiler_params=pltpu.CompilerParams(collective_id=1, has_side_effects=True, vmem_limit_bytes=VMEM_LIMIT),
         name="main_step",
     )(picks, slab, local, remote, weight, w_update, grad, pre)
@@ -308,89 +411,6 @@
     )(cols, got, tiles, gradh, feats, w_message)
 
 
-def reduce_kernel(
-    parts, slabs, factor, msg_ref, upd_ref, out_msg_ref, out_upd_ref,
-    mine_ref, in1, mid, in2, part_ref, all2, done, all1, s1, r1, s2, r2, s3, r3, s4, r4,
-):
-    b, g = lax.axis_index("blk"), lax.axis_index("grp")
-    width = msg_ref.shape[0]
-    rows = 2 * width // parts
-    barrier = pltpu.get_barrier_semaphore()
-    for k in range(1, parts):
-        pl.semaphore_signal(barrier, inc=1, device_id={"blk": lax.rem(b + k, parts)}, device_id_type=MESH)
-    for k in range(1, slabs):
-        pl.semaphore_signal(barrier, inc=1, device_id={"grp": lax.rem(g + k, slabs)}, device_id_type=MESH)
-    for k in range(parts // 2):
-        mine_ref[k] = msg_ref[k * rows : (k + 1) * rows]
-        mine_ref[parts // 2 + k] = upd_ref[k * rows : (k + 1) * rows]
-    pl.semaphore_wait(barrier, parts + slabs - 2)
-
-    def exchange(n, axis, me, src, dst, send, recv):
-        copies = []
-        for k in range(1, n):
-            peer = lax.rem(me + k, n)
-            copy = pltpu.make_async_remote_copy(
-                src(peer), dst(k), send.at[k - 1], recv.at[k - 1], device_id={axis: peer}, device_id_type=MESH
-            )
-            copy.start()
-            copies.append(copy)
-        for copy in copies:
-            copy.wait_recv()
-        return copies
-
-    sent = exchange(parts, "blk", b, lambda p: mine_ref.at[p], lambda k: in1.at[k - 1], s1, r1)
-    total = mine_ref[b]
-    for k in range(parts - 1):
-        total += in1[k]
-    for n in range(slabs):
-        mid[n] = total[n // 2 * 8 : n // 2 * 8 + 8, n % 2 * 128 : n % 2 * 128 + 128]
-    sent += exchange(slabs, "grp", g, lambda p: mid.at[p], lambda k: in2.at[k - 1], s2, r2)
-    piece = mid[g]
-    for k in range(slabs - 1):
-        piece += in2[k]
-    part_ref[...] = piece * factor
-    all2[g] = piece * factor
-    sent += exchange(slabs, "grp", g, lambda p: part_ref, lambda k: all2.at[g], s3, r3)
-    for n in range(slabs):
-        done[n // 2 * 8 : n // 2 * 8 + 8, n % 2 * 128 : n % 2 * 128 + 128] = all2[n]
-    all1[b] = done[...]
-    sent += exchange(parts, "blk", b, lambda p: done, lambda k: all1.at[b], s4, r4)
-    for k in range(parts // 2):
-        out_msg_ref[k * rows : (k + 1) * rows] = all1[k]
-        out_upd_ref[k * rows : (k + 1) * rows] = all1[parts // 2 + k]
-    for copy in sent:
-        copy.wait_send()
-
-
-def reduce_step(msg, upd, parts, slabs, factor):
-    width = msg.shape[0]
-    rows = 2 * width // parts
-    vmem = pl.BlockSpec(memory_space=pltpu.VMEM)
-    dma = pltpu.SemaphoreType.DMA
-    return pl.pallas_call(
-        functools.partial(reduce_kernel, parts, slabs, factor),
-        out_shape=[jax.ShapeDtypeStruct(msg.shape, F32)] * 2,
-        in_specs=[vmem] * 2,
-        out_specs=[vmem] * 2,
-        scratch_shapes=[
-            pltpu.VMEM((parts, rows, width), F32),
-            pltpu.VMEM((parts - 1, rows, width), F32),
-            pltpu.VMEM((slabs, 8, 128), F32),
-            pltpu.VMEM((slabs - 1, 8, 128), F32),
-            pltpu.VMEM((8, 128), F32),
-            pltpu.VMEM((slabs, 8, 128), F32),
-            pltpu.VMEM((rows, width), F32),
-            pltpu.VMEM((parts, rows, width), F32),
-            dma((parts - 1,)), dma((parts - 1,)),
-            dma((slabs - 1,)), dma((slabs - 1,)),
-            dma((slabs - 1,)), dma((slabs - 1,)),
-            dma((parts - 1,)), dma((parts - 1,)),
-        ],
-        compiler_params=pltpu.CompilerParams(collective_id=0, has_side_effects=True, vmem_limit_bytes=VMEM_LIMIT),
-        name="reduce_step",
-    )(msg, upd)
-
-
 def local(
     grad_out, pre_act, node_feats, w_message, w_update, tile_vals, tile_rows, tile_cols,
     rec_slab, rec_local, rec_remote, rec_weight,
@@ -401,14 +421,14 @@
     parts = lax.axis_size("blk")
     records = rec_local.shape[1]
     cap = 2 * records // slabs
+    factor = float((slabs * parts * rows) ** -0.5)
     lanes = lambda a: a.reshape(records // 128, 128)
     gradh, upd, got = main_step(
         tile_rows[0], lanes(rec_slab), lanes(rec_local), lanes(rec_remote), lanes(rec_weight),
-        w_update, grad, pre_act[0], slabs, parts, cap,
+        w_update, grad, pre_act[0], slabs, parts, cap, factor,
     )
     feats, msg = tile_step(tile_cols[0, 0], got, tile_vals[0, 0], gradh, node_feats[0], w_message)
-    factor = float((slabs * parts * rows) ** -0.5)
-    msg, upd = reduce_step(msg, upd, parts, slabs, factor)
+    msg = reduce_step(msg, parts, slabs, factor)
     return (feats[None], msg, upd)
 
 

time: 228 us -> 228 us (level)
    pallas_call x1, Pallas kernels: 180 us -> 184 us  [main_step(): pl.pallas_call(functools.partial(main_kernel, parts, slabs, factor), out_...]
    pallas_call x1, Pallas kernels: 31.2 us -> 27 us  [reduce_step(): pl.pallas_call(functools.partial(reduce_kernel, parts, slabs, factor), ou...]
where the time goes in v3:
time: 228 us; the launch traced here: 227 us
  Pallas kernels  224 us (98%)
  local copies, waits for them, and re-layouts  2.38 us (1%)
    pallas_call x1, Pallas kernels, main_step(): pl.pallas_call(functools.partial(main_kernel, parts, slabs, factor), out_...  184 us
    pallas_call x1, Pallas kernels, reduce_step(): pl.pallas_call(functools.partial(reduce_kernel, parts, slabs, factor), ou...  27 us
    pallas_call x1, Pallas kernels, tile_step(): pl.pallas_call(tile_kernel, grid_spec=pltpu.PrefetchScalarGridSpec(num_sc...  13.4 us

profile of v3, /device:TPU:1, one launch (start us, length us, event | category | flops | bytes accessed | tf_op | source)
XLA Modules:
  0.0 227.3 jit_solution(11866980359696494264)
XLA Ops:
  0.6 183.9 %main_step.1 = (bf16[4096,256]{1,0:T(8,128)(2,1)}, f32[256,256]{1,0:T(8,128)}, bf16[8,16,128,256]{3,2,1,0:T(8,128)(2,1)}) custom-call(s32[8,8,16]{2,1,0:T(8,128)} %bitcast.15, s32[32,128]{1,0:T(8,128)} %bitcast.16, s32[32,128]{1,0:T(8,128)} %bitcast.17, s32[32,128]{1,0:T(8,128)} %bitcast.18, f32[32,128]{1,0:T(8,128)} %bitcast.19, bf16[256,256]{1,0:T(8,128)(2,1)} %w_ref.2, ...), custom_call_target="tpu_custom_call" | custom-call | tf_op jit(solution)/shard_map/main_step/pallas_call | solution.py:333
  184.5 0.0 copy-start
  184.5 13.4 %tile_step.1 = (bf16[4096,256]{1,0:T(8,128)(2,1)}, f32[256,256]{1,0:T(8,128)}) custom-call(s32[8,16]{1,0:T(8,128)} %bitcast.20, bf16[8,16,128,256]{3,2,1,0:T(8,128)(2,1)} %get-tuple-element.8.got_ref, bf16[8,16,128,128]{3,2,1,0:T(8,128)(2,1)} %bitcast.11, bf16[4096,256]{1,0:T(8,128)(2,1)} %get-tuple-element.9.gradh_ref, bf16[4096,256]{1,0:T(8,128)(2,1)} %bitcast.12, ...), custom_call_target="tpu_custom_call" | custom-call | tf_op jit(solution)/shard_map/tile_step/pallas_call | solution.py:393
  198.0 27.0 %reduce_step.1 = f32[256,256]{1,0:T(8,128)} custom-call(f32[256,256]{1,0:T(8,128)} %get-tuple-element.11.term_ref), custom_call_target="tpu_custom_call" | custom-call | tf_op jit(solution)/shard_map/reduce_step/pallas_call | solution.py:163
  224.9 1.7 copy.17
  226.6 0.0 copy-done
  226.6 0.7 copy.18
Async XLA Ops:
  184.5 42.1 %copy-start = (f32[256,256]{1,0:T(8,128)S(1)}, f32[256,256]{1,0:T(8,128)}, u32[]{:S(2)}) copy-start(f32[256,256]{1,0:T(8,128)} %get-tuple-element.18) | copy-start | bytes 786436

commit v4 on v3

--- a/solution.py
+++ b/solution.py
@@ -71,7 +71,7 @@
 
 
 def sum_scratch(parts, slabs, width):
-    rows = width // parts
+    rows = 2 * width // parts
     dma = pltpu.SemaphoreType.DMA
     return [
         pltpu.VMEM((parts, rows, width), F32),
@@ -89,11 +89,10 @@
     ]
 
 
-def sum_stages(parts, slabs, factor, term_ref, out_ref, scratch):
+def sum_stages(parts, slabs, factor, term_refs, out_refs, scratch):
     mine, in1, mid, in2, part, all2, done, all1, s1, r1, s2, r2, s3, r3, s4, r4 = scratch
     b, g = lax.axis_index("blk"), lax.axis_index("grp")
-    width = term_ref.shape[0]
-    rows = width // parts
+    rows, half = mine.shape[1], parts // 2
     sent = []
 
     def exchange(n, axis, me, src, dst, send, recv):
@@ -110,8 +109,7 @@
 
     def begin():
         for k in range(parts):
-            mine[k] = term_ref[k * rows : (k + 1) * rows]
-        mid[...] = jnp.zeros_like(mid)
+            mine[k] = term_refs[k // half][k % half * rows : (k % half + 1) * rows]
         return exchange(parts, "blk", b, lambda p: mine.at[p], lambda k: in1.at[k - 1], s1, r1)
 
     def end(copies):
@@ -123,7 +121,7 @@
         high = rows * 2 // slabs
         spots = [(slice(n // 2 * high, (n // 2 + 1) * high), slice(n % 2 * 128, n % 2 * 128 + 128)) for n in range(slabs)]
         for n in range(slabs):
-            mid[n, :high] = total[spots[n]]
+            mid[n] = total[spots[n]]
         for copy in exchange(slabs, "grp", g, lambda p: mid.at[p], lambda k: in2.at[k - 1], s2, r2):
             copy.wait_recv()
         piece = mid[g]
@@ -134,52 +132,52 @@
         for copy in exchange(slabs, "grp", g, lambda p: part, lambda k: all2.at[g], s3, r3):
             copy.wait_recv()
         for n in range(slabs):
-            done[spots[n]] = all2[n, :high]
+            done[spots[n]] = all2[n]
         all1[b] = done[...]
         for copy in exchange(parts, "blk", b, lambda p: done, lambda k: all1.at[b], s4, r4):
             copy.wait_recv()
         for k in range(parts):
-            out_ref[k * rows : (k + 1) * rows] = all1[k]
+            out_refs[k // half][k % half * rows : (k % half + 1) * rows] = all1[k]
         for copy in sent:
             copy.wait_send()
 
     return begin, end
 
 
-def reduce_kernel(parts, slabs, factor, term_ref, out_ref, *scratch):
+def reduce_kernel(parts, slabs, factor, msg_ref, upd_ref, out_msg_ref, out_upd_ref, *scratch):
     b, g = lax.axis_index("blk"), lax.axis_index("grp")
     barrier = pltpu.get_barrier_semaphore()
     for k in range(1, parts):
         pl.semaphore_signal(barrier, inc=1, device_id={"blk": lax.rem(b + k, parts)}, device_id_type=MESH)
     for k in range(1, slabs):
         pl.semaphore_signal(barrier, inc=1, device_id={"grp": lax.rem(g + k, slabs)}, device_id_type=MESH)
-    begin, end = sum_stages(parts, slabs, factor, term_ref, out_ref, scratch)
+    begin, end = sum_stages(parts, slabs, factor, (msg_ref, upd_ref), (out_msg_ref, out_upd_ref), scratch)
     pl.semaphore_wait(barrier, parts + slabs - 2)
     end(begin())
 
 
-def reduce_step(term, parts, slabs, factor):
+def reduce_step(msg, upd, parts, slabs, factor):
     vmem = pl.BlockSpec(memory_space=pltpu.VMEM)
     return pl.pallas_call(
         functools.partial(reduce_kernel, parts, slabs, factor),
-        out_shape=jax.ShapeDtypeStruct(term.shape, F32),
-        in_specs=[vmem],
-        out_specs=vmem,
-        scratch_shapes=sum_scratch(parts, slabs, term.shape[0]),
+        out_shape=[jax.ShapeDtypeStruct(msg.shape, F32)] * 2,
+        in_specs=[vmem] * 2,
+        out_specs=[vmem] * 2,
+        scratch_shapes=sum_scratch(parts, slabs, msg.shape[0]),
         compiler_params=pltpu.CompilerParams(collective_id=0, has_side_effects=True, vmem_limit_bytes=VMEM_LIMIT),
         name="reduce_step",
-    )(term)
+    )(msg, upd)
 
 
 FAR = ((2, 1), (1, 1), (3, 1), (0, 1), (2, 0), (1, 0), (3, 0))
 
 
 def main_kernel(
-    parts, slabs, factor,
+    parts, slabs,
     picks_ref, slab_ref, local_ref, remote_ref, weight_ref, w_ref, grad_hbm, pre_hbm,
     gradh_hbm, upd_ref, got_hbm,
     node_ref, scale_ref, ext_ref, out_buf, in_buf, grad_ref, pre_ref, gradh_ref, acc_ref, gp_ref, stage_ref,
-    load_sem, rec_send, rec_recv, blk_send, blk_recv, store_sem, term_ref, *scratch,
+    load_sem, rec_send, rec_recv, blk_send, blk_recv, store_sem,
 ):
     b, g = lax.axis_index("blk"), lax.axis_index("grp")
     y, xh = b // 2, b % 2
@@ -276,7 +274,7 @@
     lax.fori_loop(0, slabs, scatter, 0)
 
     load_pre.wait()
-    term_ref[...] = jnp.zeros_like(term_ref)
+    upd_ref[...] = jnp.zeros_like(upd_ref)
 
     def finish(i, _):
         at = pl.ds(pl.multiple_of(i * 256, 256), 256)
@@ -288,14 +286,12 @@
         slope = sig * (1.0 + pre * (1.0 - sig))
         back = lax.dot_general(gradh, w_ref[...], NT, preferred_element_type=F32)
         gp_ref[pl.ds(i * 2, 2)] = (back * slope).astype(BF16).reshape(2, 128, width)
-        term_ref[...] += lax.dot_general(act, gradh, TN, preferred_element_type=F32)
+        upd_ref[...] += lax.dot_general(act, gradh, TN, preferred_element_type=F32)
         return 0
 
     lax.fori_loop(0, nodes // 256, finish, 0)
     store_gradh = pltpu.make_async_copy(gradh_ref, gradh_hbm, store_sem.at[0])
     store_gradh.start()
-    begin, end = sum_stages(parts, slabs, factor, term_ref, upd_ref, scratch)
-    first = begin()
 
     def pack(n, c):
         def one(t, _):
@@ -316,7 +312,6 @@
     pack(parts - 1, b)
     keep = pltpu.make_async_copy(stage_ref.at[parts - 1], got_hbm.at[b], store_sem.at[1])
     keep.start()
-    end(first)
     lax.fori_loop(0, slabs - 1, lambda n, x: (rec_copy(n).wait_send(), x)[1], 0)
     for copy in sends:
         copy.wait()
@@ -324,14 +319,14 @@
     store_gradh.wait()
 
 
-def main_step(picks, slab, local, remote, weight, w_update, grad, pre, slabs, parts, cap, factor):
+def main_step(picks, slab, local, remote, weight, w_update, grad, pre, slabs, parts, cap):
     nodes, width = grad.shape
     count = picks.shape[-1]
     vmem = pl.BlockSpec(memory_space=pltpu.VMEM)
     hbm = pl.BlockSpec(memory_space=pl.ANY)
     dma = pltpu.SemaphoreType.DMA
     return pl.pallas_call(
-        functools.partial(main_kernel, parts, slabs, factor),
+        functools.partial(main_kernel, parts, slabs),
         out_shape=[
             jax.ShapeDtypeStruct((nodes, width), BF16),
             jax.ShapeDtypeStruct((width, width), F32),
@@ -352,9 +347,7 @@
             pltpu.VMEM((nodes // 128, 128, width), BF16),
             pltpu.VMEM((parts, count, 128, width), BF16),
             dma((2,)), dma((slabs - 1,)), dma((slabs,)), dma((parts - 1,)), dma((parts - 1,)), dma((2,)),
-            pltpu.VMEM((width, width), F32),
-        ]
-        + sum_scratch(parts, slabs, width),
+        ],
         compiler_params=pltpu.CompilerParams(collective_id=1, has_side_effects=True, vmem_limit_bytes=VMEM_LIMIT),
         name="main_step",
     )(picks, slab, local, remote, weight, w_update, grad, pre)
@@ -425,10 +418,10 @@
     lanes = lambda a: a.reshape(records // 128, 128)
     gradh, upd, got = main_step(
         tile_rows[0], lanes(rec_slab), lanes(rec_local), lanes(rec_remote), lanes(rec_weight),
-        w_update, grad, pre_act[0], slabs, parts, cap, factor,
+        w_update, grad, pre_act[0], slabs, parts, cap,
     )
     feats, msg = tile_step(tile_cols[0, 0], got, tile_vals[0, 0], gradh, node_feats[0], w_message)
-    msg = reduce_step(msg, parts, slabs, factor)
+    msg, upd = reduce_step(msg, upd, parts, slabs, factor)
     return (feats[None], msg, upd)
 
 

time: 228 us -> 219 us (0.961)
  Pallas kernels: 224 us -> 215 us
    pallas_call x1, Pallas kernels: 184 us -> 170 us  [main_step(): pl.pallas_call(functools.partial(main_kernel, parts, slabs), out_shape=[j...]
    pallas_call x1, Pallas kernels: 27 us -> 31.2 us  [reduce_step(): pl.pallas_call(functools.partial(reduce_kernel, parts, slabs, factor), ou...]
where the time goes in v4:
time: 219 us
  Pallas kernels  215 us (98%)
  local copies, waits for them, and re-layouts  3.34 us (2%)
    pallas_call x1, Pallas kernels, main_step(): pl.pallas_call(functools.partial(main_kernel, parts, slabs), out_shape=[j...  170 us
    pallas_call x1, Pallas kernels, reduce_step(): pl.pallas_call(functools.partial(reduce_kernel, parts, slabs, factor), ou...  31.2 us
    pallas_call x1, Pallas kernels, tile_step(): pl.pallas_call(tile_kernel, grid_spec=pltpu.PrefetchScalarGridSpec(num_sc...  13.3 us

profile of v4, /device:TPU:1, one launch (start us, length us, event | category | flops | bytes accessed | tf_op | source)
XLA Modules:
  0.0 218.8 jit_solution(2095347575043169754)
XLA Ops:
  0.6 170.2 %main_step.1 = (bf16[4096,256]{1,0:T(8,128)(2,1)}, f32[256,256]{1,0:T(8,128)}, bf16[8,16,128,256]{3,2,1,0:T(8,128)(2,1)}) custom-call(s32[8,8,16]{2,1,0:T(8,128)} %bitcast.15, s32[32,128]{1,0:T(8,128)} %bitcast.16, s32[32,128]{1,0:T(8,128)} %bitcast.17, s32[32,128]{1,0:T(8,128)} %bitcast.18, f32[32,128]{1,0:T(8,128)} %bitcast.19, bf16[256,256]{1,0:T(8,128)(2,1)} %w_ref.2, ...), custom_call_target="tpu_custom_call" | custom-call | tf_op jit(solution)/shard_map/main_step/pallas_call | solution.py:328
  170.9 13.3 %tile_step.1 = (bf16[4096,256]{1,0:T(8,128)(2,1)}, f32[256,256]{1,0:T(8,128)}) custom-call(s32[8,16]{1,0:T(8,128)} %bitcast.20, bf16[8,16,128,256]{3,2,1,0:T(8,128)(2,1)} %get-tuple-element.10.got_ref, bf16[8,16,128,128]{3,2,1,0:T(8,128)(2,1)} %bitcast.11, bf16[4096,256]{1,0:T(8,128)(2,1)} %get-tuple-element.11.gradh_ref, bf16[4096,256]{1,0:T(8,128)(2,1)} %bitcast.12, ...), custom_call_target="tpu_custom_call" | custom-call | tf_op jit(solution)/shard_map/tile_step/pallas_call | solution.py:386
  184.2 31.2 %reduce_step.1 = (f32[256,256]{1,0:T(8,128)}, f32[256,256]{1,0:T(8,128)}) custom-call(f32[256,256]{1,0:T(8,128)} %get-tuple-element.13.msg_ref, f32[256,256]{1,0:T(8,128)} %get-tuple-element.14.upd_ref), custom_call_target="tpu_custom_call" | custom-call | tf_op jit(solution)/shard_map/reduce_step/pallas_call | solution.py:161
  215.4 1.7 copy.17
  217.1 1.7 copy.18

commit v5 on v4

--- a/solution.py
+++ b/solution.py
@@ -13,7 +13,7 @@
 NT = (((1,), (1,)), ((), ()))
 TN = (((0,), (0,)), ((), ()))
 EXT = 16
-VMEM_LIMIT = 56 * 1024 * 1024
+VMEM_LIMIT = 61 * 1024 * 1024
 
 
 def iota(shape, dim):
@@ -144,53 +144,50 @@
     return begin, end
 
 
-def reduce_kernel(parts, slabs, factor, msg_ref, upd_ref, out_msg_ref, out_upd_ref, *scratch):
-    b, g = lax.axis_index("blk"), lax.axis_index("grp")
-    barrier = pltpu.get_barrier_semaphore()
-    for k in range(1, parts):
-        pl.semaphore_signal(barrier, inc=1, device_id={"blk": lax.rem(b + k, parts)}, device_id_type=MESH)
-    for k in range(1, slabs):
-        pl.semaphore_signal(barrier, inc=1, device_id={"grp": lax.rem(g + k, slabs)}, device_id_type=MESH)
-    begin, end = sum_stages(parts, slabs, factor, (msg_ref, upd_ref), (out_msg_ref, out_upd_ref), scratch)
-    pl.semaphore_wait(barrier, parts + slabs - 2)
-    end(begin())
-
-
-def reduce_step(msg, upd, parts, slabs, factor):
-    vmem = pl.BlockSpec(memory_space=pltpu.VMEM)
-    return pl.pallas_call(
-        functools.partial(reduce_kernel, parts, slabs, factor),
-        out_shape=[jax.ShapeDtypeStruct(msg.shape, F32)] * 2,
-        in_specs=[vmem] * 2,
-        out_specs=[vmem] * 2,
-        scratch_shapes=sum_scratch(parts, slabs, msg.shape[0]),
-        compiler_params=pltpu.CompilerParams(collective_id=0, has_side_effects=True, vmem_limit_bytes=VMEM_LIMIT),
-        name="reduce_step",
-    )(msg, upd)
+def column_order(cols_ref, order_ref):
+    count = cols_ref.shape[1]
+    cols = jnp.broadcast_to(cols_ref[...].astype(F32), (count, count))
+    across, down = iota((count, count), 1).astype(F32), iota((count, count), 0).astype(F32)
+    turned = jnp.transpose(cols)
+    ones = lambda hit: jnp.where(hit, 1.0, 0.0)
+    total = lambda x: jnp.sum(x, axis=0, keepdims=True)
+    rank = total(ones(turned * count + down < cols * count + across))
+    ranks = jnp.transpose(jnp.broadcast_to(rank, (count, count)))
+    hit = ones(ranks == across)
+    order = total(hit * down)
+    here = total(hit * turned)
+    before = total(ones(ranks == across - 1.0) * (turned + 1.0)) - 1.0
+    last = jnp.maximum(total(ones(turned <= across)) - 1.0, 0.0)
+    named = jnp.minimum(total(ones(turned == across)), 1.0)
+    rows = [order, ones(here == before), last, named, jnp.zeros((4, count), F32)]
+    order_ref[...] = jnp.concatenate(rows, axis=0).astype(jnp.int32)
 
 
 FAR = ((2, 1), (1, 1), (3, 1), (0, 1), (2, 0), (1, 0), (3, 0))
 
 
 def main_kernel(
-    parts, slabs,
-    picks_ref, slab_ref, local_ref, remote_ref, weight_ref, w_ref, grad_hbm, pre_hbm,
-    gradh_hbm, upd_ref, got_hbm,
-    node_ref, scale_ref, ext_ref, out_buf, in_buf, grad_ref, pre_ref, gradh_ref, acc_ref, gp_ref, stage_ref,
-    load_sem, rec_send, rec_recv, blk_send, blk_recv, store_sem,
+    parts, slabs, factor,
+    picks_ref, slab_ref, local_ref, remote_ref, weight_ref, cols_ref, w_ref, grad_hbm, pre_hbm, feats_hbm, tiles_hbm,
+    gradh_hbm, spread_hbm, out_msg_ref, out_upd_ref,
+    node_ref, scale_ref, ext_ref, out_buf, in_buf, grad_ref, pre_ref, acc_ref, gp_ref, stage_ref, got_ref,
+    tiles_ref, run_ref, turned_ref, order_ref, order_smem, msg_ref, upd_ref,
+    load_sem, rec_send, rec_recv, blk_send, blk_recv, store_sem, *scratch,
 ):
     b, g = lax.axis_index("blk"), lax.axis_index("grp")
     y, xh = b // 2, b % 2
     xl, z, core = g // 8, (g // 2) % 4, g % 2
     cap = node_ref.shape[1]
-    half = cap // 2
     nodes, width = acc_ref.shape
     picks = stage_ref.shape[1]
 
     load_grad = pltpu.make_async_copy(grad_hbm, grad_ref, load_sem.at[0])
     load_pre = pltpu.make_async_copy(pre_hbm, pre_ref, load_sem.at[1])
+    load_tiles = pltpu.make_async_copy(tiles_hbm, tiles_ref, load_sem.at[2])
+    load_feats = pltpu.make_async_copy(feats_hbm, pre_ref, load_sem.at[3])
     load_grad.start()
     load_pre.start()
+    load_tiles.start()
 
     def rec_peer(n):
         q = n // 4
@@ -279,7 +276,7 @@
     def finish(i, _):
         at = pl.ds(pl.multiple_of(i * 256, 256), 256)
         gradh = acc_ref[at].astype(BF16)
-        gradh_ref[at] = gradh
+        grad_ref[at] = gradh
         pre = pre_ref[at].astype(F32)
         sig = 1.0 / (1.0 + jnp.exp(-pre))
         act = (pre * sig).astype(BF16)
@@ -290,50 +287,96 @@
         return 0
 
     lax.fori_loop(0, nodes // 256, finish, 0)
-    store_gradh = pltpu.make_async_copy(gradh_ref, gradh_hbm, store_sem.at[0])
+    load_feats.start()
+    store_gradh = pltpu.make_async_copy(grad_ref, gradh_hbm, store_sem.at[0])
     store_gradh.start()
 
-    def pack(n, c):
+    def pack(to_ref, at, c):
         def one(t, _):
-            stage_ref[n, t] = gp_ref[picks_ref[c, b, t]]
+            to_ref[at + t] = gp_ref[picks_ref[c, b, t]]
             return 0
 
         lax.fori_loop(0, picks, one, 0)
 
     sends = []
     for n in range(parts - 1):
-        pack(n, blk_peer(n))
+        pack(stage_ref.at[n], 0, blk_peer(n))
         copy = pltpu.make_async_remote_copy(
-            stage_ref.at[n], got_hbm.at[b], blk_send.at[n], blk_recv.at[n],
+            stage_ref.at[n], got_ref.at[pl.ds(b * picks, picks)], blk_send.at[n], blk_recv.at[n],
             device_id={"blk": blk_peer(n)}, device_id_type=MESH,
         )
         copy.start()
         sends.append(copy)
-    pack(parts - 1, b)
-    keep = pltpu.make_async_copy(stage_ref.at[parts - 1], got_hbm.at[b], store_sem.at[1])
-    keep.start()
+    pack(got_ref, b * picks, b)
+
+    column_order(cols_ref, order_ref)
+    to_smem = pltpu.make_async_copy(order_ref, order_smem, store_sem.at[1])
+    to_smem.start()
+    load_tiles.wait()
+    tiles = parts * picks
+
+    def turn(k, _):
+        tiles_ref[k] = jnp.transpose(tiles_ref[k])
+        return 0
+
+    lax.fori_loop(0, tiles, turn, 0)
+    load_feats.wait()
+
+    def turn_feats(k, _):
+        at = pl.ds(pl.multiple_of(k * 256, 256), 256)
+        turned_ref[k] = jnp.transpose(pre_ref[at])
+        return 0
+
+    lax.fori_loop(0, nodes // 256, turn_feats, 0)
+    to_smem.wait()
     lax.fori_loop(0, slabs - 1, lambda n, x: (rec_copy(n).wait_send(), x)[1], 0)
+    store_gradh.wait()
     for copy in sends:
         copy.wait()
-    keep.wait()
-    store_gradh.wait()
-
-
-def main_step(picks, slab, local, remote, weight, w_update, grad, pre, slabs, parts, cap):
+
+    group = 8
+
+    def products(m, total):
+        for q in range(group):
+            k = m * group + q
+            f = lax.clamp(0, order_smem[0, k], tiles - 1)
+            part = jnp.dot(tiles_ref[f], got_ref[f], preferred_element_type=F32)
+            total = total * order_smem[1, k].astype(F32) + part
+            run_ref[k] = total.astype(BF16)
+        return total
+
+    lax.fori_loop(0, tiles // group, products, jnp.zeros((128, width), F32))
+
+    def settle(j, _):
+        last = run_ref[lax.clamp(0, order_smem[2, j], tiles - 1)]
+        gp_ref[j] = (last.astype(F32) * order_smem[3, j].astype(F32)).astype(BF16)
+        return 0
+
+    lax.fori_loop(0, nodes // 128, settle, 0)
+    store_spread = pltpu.make_async_copy(gp_ref, spread_hbm, store_sem.at[2])
+    store_spread.start()
+    msg = jnp.zeros((width, width), F32)
+    for k in range(nodes // 256):
+        msg += jnp.dot(turned_ref[k], gp_ref[2 * k : 2 * k + 2].reshape(256, width), preferred_element_type=F32)
+    msg_ref[...] = msg
+    begin, end = sum_stages(parts, slabs, factor, (msg_ref, upd_ref), (out_msg_ref, out_upd_ref), scratch)
+    end(begin())
+    store_spread.wait()
+
+
+def main_step(picks, slab, local, remote, weight, cols, w_update, grad, pre, feats, tiles, slabs, parts, cap, factor):
     nodes, width = grad.shape
     count = picks.shape[-1]
     vmem = pl.BlockSpec(memory_space=pltpu.VMEM)
     hbm = pl.BlockSpec(memory_space=pl.ANY)
     dma = pltpu.SemaphoreType.DMA
+    panels = jax.ShapeDtypeStruct((nodes // 128, 128, width), BF16)
+    square = jax.ShapeDtypeStruct((width, width), F32)
     return pl.pallas_call(
-        functools.partial(main_kernel, parts, slabs),
-        out_shape=[
-            jax.ShapeDtypeStruct((nodes, width), BF16),
-            jax.ShapeDtypeStruct((width, width), F32),
-            jax.ShapeDtypeStruct((parts, count, 128, width), BF16),
-        ],
-        in_specs=[pl.BlockSpec(memory_space=pltpu.SMEM)] + [vmem] * 5 + [hbm] * 2,
-        out_specs=[hbm, vmem, hbm],
+        functools.partial(main_kernel, parts, slabs, factor),
+        out_shape=[jax.ShapeDtypeStruct((nodes, width), BF16), panels, square, square],
+        in_specs=[pl.BlockSpec(memory_space=pltpu.SMEM)] + [vmem] * 6 + [hbm] * 4,
+        out_specs=[hbm, hbm, vmem, vmem],
         scratch_shapes=[
             pltpu.VMEM((slabs, cap, 128), jnp.int32),
             pltpu.VMEM((slabs, cap, 128), F32),
@@ -342,66 +385,49 @@
             pltpu.VMEM((slabs, cap + EXT, width), BF16),
             pltpu.VMEM((nodes, width), BF16),
             pltpu.VMEM((nodes, width), BF16),
-            pltpu.VMEM((nodes, width), BF16),
             pltpu.VMEM((nodes, width), F32),
             pltpu.VMEM((nodes // 128, 128, width), BF16),
-            pltpu.VMEM((parts, count, 128, width), BF16),
-            dma((2,)), dma((slabs - 1,)), dma((slabs,)), dma((parts - 1,)), dma((parts - 1,)), dma((2,)),
-        ],
-        compiler_params=pltpu.CompilerParams(collective_id=1, has_side_effects=True, vmem_limit_bytes=VMEM_LIMIT),
+            pltpu.VMEM((parts - 1, count, 128, width), BF16),
+            pltpu.VMEM((parts * count, 128, width), BF16),
+            pltpu.VMEM((parts * count, 128, 128), BF16),
+            pltpu.VMEM((parts * count, 128, width), BF16),
+            pltpu.VMEM((nodes // 256, width, 256), BF16),
+            pltpu.VMEM((8, parts * count), jnp.int32),
+            pltpu.SMEM((8, parts * count), jnp.int32),
+            pltpu.VMEM((width, width), F32),
+            pltpu.VMEM((width, width), F32),
+            dma((4,)), dma((slabs - 1,)), dma((slabs,)), dma((parts - 1,)), dma((parts - 1,)), dma((3,)),
+        ]
+        + sum_scratch(parts, slabs, width),
+        compiler_params=pltpu.CompilerParams(collective_id=0, has_side_effects=True, vmem_limit_bytes=VMEM_LIMIT),
         name="main_step",
-    )(picks, slab, local, remote, weight, w_update, grad, pre)
-
-
-def tile_kernel(cols_ref, got_ref, tiles_ref, gradh_ref, feats_ref, w_ref, out_ref, msg_ref, total_ref):
-    r = pl.program_id(0)
-    picks = got_ref.shape[1]
-
-    @pl.when(r == 0)
+    )(picks, slab, local, remote, weight, cols, w_update, grad, pre, feats, tiles)
+
+
+def final_kernel(gradh_ref, spread_ref, w_ref, msg_ref, upd_ref, out_ref, out_msg_ref, out_upd_ref):
+    down = lax.dot_general(spread_ref[...], w_ref[...], NT, preferred_element_type=F32)
+    out_ref[...] = (gradh_ref[...].astype(F32) + down).astype(BF16)
+
+    @pl.when(pl.program_id(0) == 0)
     def _():
-        total_ref[...] = jnp.zeros_like(total_ref)
-
-    for t in range(picks):
-        part = lax.dot_general(tiles_ref[0, t], got_ref[0, t], TN, preferred_element_type=F32)
-        at = pl.ds(pl.multiple_of(cols_ref[r, t] * 128, 128), 128)
-        total_ref[at] += part
-
-    @pl.when(r == pl.num_programs(0) - 1)
-    def _():
-        msg = jnp.zeros(msg_ref.shape, F32)
-        tall = 512
-        for k in range(total_ref.shape[0] // tall):
-            at = slice(k * tall, (k + 1) * tall)
-            spread = total_ref[at].astype(BF16)
-            msg += lax.dot_general(feats_ref[at], spread, TN, preferred_element_type=F32)
-            down = lax.dot_general(spread, w_ref[...], NT, preferred_element_type=F32)
-            out_ref[at] = (gradh_ref[at].astype(F32) + down).astype(BF16)
-        msg_ref[...] = msg
-
-
-def tile_step(cols, got, tiles, gradh, feats, w_message):
-    parts, picks = cols.shape
+        out_msg_ref[...] = msg_ref[...]
+        out_upd_ref[...] = upd_ref[...]
+
+
+def final_step(gradh, spread, w_message, msg, upd):
     rows, width = gradh.shape
-    whole = lambda a: pl.BlockSpec(a.shape, lambda i, *_: (0,) * a.ndim)
+    tall = rows // 4
+    tile = pl.BlockSpec((tall, width), lambda i: (i, 0))
+    square = pl.BlockSpec((width, width), lambda i: (0, 0))
     return pl.pallas_call(
-        tile_kernel,
-        grid_spec=pltpu.PrefetchScalarGridSpec(
-            num_scalar_prefetch=1,
-            grid=(parts,),
-            in_specs=[
-                pl.BlockSpec((1, picks, 128, width), lambda i, *_: (i, 0, 0, 0)),
-                pl.BlockSpec((1, picks, 128, 128), lambda i, *_: (i, 0, 0, 0)),
-                whole(gradh),
-                whole(feats),
-                whole(w_message),
-            ],
-            out_specs=[whole(gradh), pl.BlockSpec((width, width), lambda i, *_: (0, 0))],
-            scratch_shapes=[pltpu.VMEM((rows, width), F32)],
-        ),
-        out_shape=[jax.ShapeDtypeStruct((rows, width), BF16), jax.ShapeDtypeStruct((width, width), F32)],
+        final_kernel,
+        grid=(rows // tall,),
+        out_shape=[jax.ShapeDtypeStruct(gradh.shape, BF16)] + [jax.ShapeDtypeStruct(msg.shape, F32)] * 2,
+        in_specs=[tile, tile, square, square, square],
+        out_specs=[tile, square, square],
         compiler_params=pltpu.CompilerParams(vmem_limit_bytes=VMEM_LIMIT),
-        name="tile_step",
-    )(cols, got, tiles, gradh, feats, w_message)
+        name="final_step",
+    )(gradh, spread, w_message, msg, upd)
 
 
 def local(
@@ -416,12 +442,14 @@
     cap = 2 * records // slabs
     factor = float((slabs * parts * rows) ** -0.5)
     lanes = lambda a: a.reshape(records // 128, 128)
-    gradh, upd, got = main_step(
+    tiles = tile_vals[0, 0]
+    count = tiles.shape[0] * tiles.shape[1]
+    gradh, spread, msg, upd = main_step(
         tile_rows[0], lanes(rec_slab), lanes(rec_local), lanes(rec_remote), lanes(rec_weight),
-        w_update, grad, pre_act[0], slabs, parts, cap,
+        tile_cols[0, 0].reshape(1, count), w_update, grad, pre_act[0], node_feats[0],
+        tiles.reshape(count, *tiles.shape[2:]), slabs, parts, cap, factor,
     )
-    feats, msg = tile_step(tile_cols[0, 0], got, tile_vals[0, 0], gradh, node_feats[0], w_message)
-    msg, upd = reduce_step(msg, upd, parts, slabs, factor)
+    feats, msg, upd = final_step(gradh, spread.reshape(rows, width), w_message, msg, upd)
     return (feats[None], msg, upd)
 
 

time: 219 us -> 209 us (0.954)
  Pallas kernels: 215 us -> 207 us
    pallas_call x3 -> x2, Pallas kernels: 215 us -> 207 us  [the longest x1 202 us: main_step(): pl.pallas_call(functools.partial(main_kernel, parts, slabs, factor), out_...]
    unnamed x2 -> x0, local copies, waits for them, and re-layouts: 3.34 us -> none
where the time goes in v5:
time: 209 us
  Pallas kernels  207 us (99%)
    pallas_call x1, Pallas kernels, main_step(): pl.pallas_call(functools.partial(main_kernel, parts, slabs, factor), out_...  202 us
    pallas_call x1, Pallas kernels, final_step(): pl.pallas_call(final_kernel, grid=(rows // tall,), out_shape=[jax.ShapeDt...  5.13 us

profile of v5, /device:TPU:1, one launch (start us, length us, event | category | flops | bytes accessed | tf_op | source)
XLA Modules:
  0.0 209.2 jit_solution(6479559364992505494)
XLA Ops:
  0.6 1.3 reshape_squeeze.6.cols_ref
  1.9 202.1 %main_step.1 = (bf16[4096,256]{1,0:T(8,128)(2,1)}, bf16[32,128,256]{2,1,0:T(8,128)(2,1)}, f32[256,256]{1,0:T(8,128)}, f32[256,256]{1,0:T(8,128)}) custom-call(s32[8,8,16]{2,1,0:T(8,128)} %bitcast.18, s32[32,128]{1,0:T(8,128)} %bitcast.19, s32[32,128]{1,0:T(8,128)} %bitcast.20, s32[32,128]{1,0:T(8,128)} %bitcast.21, f32[32,128]{1,0:T(8,128)} %bitcast.22, ...), custom_call_target="tpu_custom_call" | custom-call | tf_op jit(solution)/shard_map/main_step/pallas_call | solution.py:375
  204.0 5.1 %final_step.1 = (bf16[4096,256]{1,0:T(8,128)(2,1)}, f32[256,256]{1,0:T(8,128)}, f32[256,256]{1,0:T(8,128)}) custom-call(bf16[4096,256]{1,0:T(8,128)(2,1)} %get-tuple-element.10.gradh_ref, bf16[4096,256]{1,0:T(8,128)(2,1)} %bitcast.14, bf16[256,256]{1,0:T(8,128)(2,1)} %w_ref.3, f32[256,256]{1,0:T(8,128)} %get-tuple-element.12.msg_ref, ...), custom_call_target="tpu_custom_call" | custom-call | tf_op jit(solution)/shard_map/final_step/pallas_call | solution.py:422

commit v6 on v5

--- a/solution.py
+++ b/solution.py
@@ -71,7 +71,7 @@
 
 
 def sum_scratch(parts, slabs, width):
-    rows = 2 * width // parts
+    rows = width // parts
     dma = pltpu.SemaphoreType.DMA
     return [
         pltpu.VMEM((parts, rows, width), F32),
@@ -89,11 +89,13 @@
     ]
 
 
-def sum_stages(parts, slabs, factor, term_refs, out_refs, scratch):
+def sum_stages(parts, slabs, factor, term_ref, out_ref, scratch):
     mine, in1, mid, in2, part, all2, done, all1, s1, r1, s2, r2, s3, r3, s4, r4 = scratch
     b, g = lax.axis_index("blk"), lax.axis_index("grp")
-    rows, half = mine.shape[1], parts // 2
-    sent = []
+    rows = mine.shape[1]
+    high = rows * 2 // slabs
+    spots = [(slice(n // 2 * high, (n // 2 + 1) * high), slice(n % 2 * 128, n % 2 * 128 + 128)) for n in range(slabs)]
+    flights = []
 
     def exchange(n, axis, me, src, dst, send, recv):
         copies = []
@@ -104,49 +106,61 @@
             )
             copy.start()
             copies.append(copy)
-        sent.extend(copies)
-        return copies
-
-    def begin():
+        flights.append(copies)
+
+    def landed():
+        for copy in flights[-1]:
+            copy.wait_recv()
+
+    def split_blk():
+        mid[...] = jnp.zeros_like(mid)
         for k in range(parts):
-            mine[k] = term_refs[k // half][k % half * rows : (k % half + 1) * rows]
-        return exchange(parts, "blk", b, lambda p: mine.at[p], lambda k: in1.at[k - 1], s1, r1)
-
-    def end(copies):
-        for copy in copies:
-            copy.wait_recv()
+            mine[k] = term_ref[k * rows : (k + 1) * rows]
+        exchange(parts, "blk", b, lambda p: mine.at[p], lambda k: in1.at[k - 1], s1, r1)
+
+    def split_grp():
+        landed()
         total = mine[b]
         for k in range(parts - 1):
             total += in1[k]
-        high = rows * 2 // slabs
-        spots = [(slice(n // 2 * high, (n // 2 + 1) * high), slice(n % 2 * 128, n % 2 * 128 + 128)) for n in range(slabs)]
         for n in range(slabs):
-            mid[n] = total[spots[n]]
-        for copy in exchange(slabs, "grp", g, lambda p: mid.at[p], lambda k: in2.at[k - 1], s2, r2):
-            copy.wait_recv()
+            mid[n, :high] = total[spots[n]]
+        exchange(slabs, "grp", g, lambda p: mid.at[p], lambda k: in2.at[k - 1], s2, r2)
+
+    def join_grp():
+        landed()
         piece = mid[g]
         for k in range(slabs - 1):
             piece += in2[k]
         part[...] = piece * factor
         all2[g] = piece * factor
-        for copy in exchange(slabs, "grp", g, lambda p: part, lambda k: all2.at[g], s3, r3):
-            copy.wait_recv()
+        exchange(slabs, "grp", g, lambda p: part, lambda k: all2.at[g], s3, r3)
+
+    def join_blk():
+        landed()
         for n in range(slabs):
-            done[spots[n]] = all2[n]
+            done[spots[n]] = all2[n, :high]
         all1[b] = done[...]
-        for copy in exchange(parts, "blk", b, lambda p: done, lambda k: all1.at[b], s4, r4):
-            copy.wait_recv()
+        exchange(parts, "blk", b, lambda p: done, lambda k: all1.at[b], s4, r4)
+
+    def finish():
+        landed()
         for k in range(parts):
-            out_refs[k // half][k % half * rows : (k % half + 1) * rows] = all1[k]
-        for copy in sent:
-            copy.wait_send()
-
-    return begin, end
+            out_ref[k * rows : (k + 1) * rows] = all1[k]
+        for copies in flights:
+            for copy in copies:
+                copy.wait_send()
+
+    return split_blk, split_grp, join_grp, join_blk, finish
 
 
 def column_order(cols_ref, order_ref):
-    count = cols_ref.shape[1]
-    cols = jnp.broadcast_to(cols_ref[...].astype(F32), (count, count))
+    parts, picks = cols_ref.shape
+    count = parts * picks
+    repeat = jnp.where(iota((picks, count), 1) % picks == iota((picks, count), 0), 1.0, 0.0).astype(BF16)
+    wide = jnp.dot(cols_ref[...].astype(F32).astype(BF16), repeat, preferred_element_type=F32)
+    own = jnp.where(iota((parts, count), 1) // picks == iota((parts, count), 0), wide, 0.0)
+    cols = jnp.broadcast_to(jnp.sum(own, axis=0, keepdims=True), (count, count))
     across, down = iota((count, count), 1).astype(F32), iota((count, count), 0).astype(F32)
     turned = jnp.transpose(cols)
     ones = lambda hit: jnp.where(hit, 1.0, 0.0)
@@ -334,6 +348,10 @@
     for copy in sends:
         copy.wait()
 
+    half = len(scratch) // 2
+    upd_sum = sum_stages(parts, slabs, factor, upd_ref, out_upd_ref, scratch[:half])
+    msg_sum = sum_stages(parts, slabs, factor, msg_ref, out_msg_ref, scratch[half:])
+    upd_sum[0]()
     group = 8
 
     def products(m, total):
@@ -355,12 +373,19 @@
     lax.fori_loop(0, nodes // 128, settle, 0)
     store_spread = pltpu.make_async_copy(gp_ref, spread_hbm, store_sem.at[2])
     store_spread.start()
+    upd_sum[1]()
     msg = jnp.zeros((width, width), F32)
     for k in range(nodes // 256):
         msg += jnp.dot(turned_ref[k], gp_ref[2 * k : 2 * k + 2].reshape(256, width), preferred_element_type=F32)
     msg_ref[...] = msg
-    begin, end = sum_stages(parts, slabs, factor, (msg_ref, upd_ref), (out_msg_ref, out_upd_ref), scratch)
-    end(begin())
+    msg_sum[0]()
+    upd_sum[2]()
+    msg_sum[1]()
+    upd_sum[3]()
+    msg_sum[2]()
+    msg_sum[3]()
+    upd_sum[4]()
+    msg_sum[4]()
     store_spread.wait()
 
 
@@ -398,7 +423,7 @@
             pltpu.VMEM((width, width), F32),
             dma((4,)), dma((slabs - 1,)), dma((slabs,)), dma((parts - 1,)), dma((parts - 1,)), dma((3,)),
         ]
-        + sum_scratch(parts, slabs, width),
+        + sum_scratch(parts, slabs, width) * 2,
         compiler_params=pltpu.CompilerParams(collective_id=0, has_side_effects=True, vmem_limit_bytes=VMEM_LIMIT),
         name="main_step",
     )(picks, slab, local, remote, weight, cols, w_update, grad, pre, feats, tiles)
@@ -446,7 +471,7 @@
     count = tiles.shape[0] * tiles.shape[1]
     gradh, spread, msg, upd = main_step(
         tile_rows[0], lanes(rec_slab), lanes(rec_local), lanes(rec_remote), lanes(rec_weight),
-        tile_cols[0, 0].reshape(1, count), w_update, grad, pre_act[0], node_feats[0],
+        tile_cols[0, 0], w_update, grad, pre_act[0], node_feats[0],
         tiles.reshape(count, *tiles.shape[2:]), slabs, parts, cap, factor,
     )
     feats, msg, upd = final_step(gradh, spread.reshape(rows, width), w_message, msg, upd)

time: 209 us -> 205 us (0.981)
  Pallas kernels: 207 us -> 204 us
    pallas_call x1, Pallas kernels: 202 us -> 199 us  [main_step(): pl.pallas_call(functools.partial(main_kernel, parts, slabs, factor), out_...]
where the time goes in v6:
time: 205 us
  Pallas kernels  204 us (100%)
    pallas_call x1, Pallas kernels, main_step(): pl.pallas_call(functools.partial(main_kernel, parts, slabs, factor), out_...  199 us
    pallas_call x1, Pallas kernels, final_step(): pl.pallas_call(final_kernel, grid=(rows // tall,), out_shape=[jax.ShapeDt...  5.13 us

profile of v6, /device:TPU:1, one launch (start us, length us, event | category | flops | bytes accessed | tf_op | source)
XLA Modules:
  0.0 205.0 jit_solution(14450723442013232152)
XLA Ops:
  0.6 199.2 %main_step.1 = (bf16[4096,256]{1,0:T(8,128)(2,1)}, bf16[32,128,256]{2,1,0:T(8,128)(2,1)}, f32[256,256]{1,0:T(8,128)}, f32[256,256]{1,0:T(8,128)}) custom-call(s32[8,8,16]{2,1,0:T(8,128)} %bitcast.17, s32[32,128]{1,0:T(8,128)} %bitcast.18, s32[32,128]{1,0:T(8,128)} %bitcast.19, s32[32,128]{1,0:T(8,128)} %bitcast.20, f32[32,128]{1,0:T(8,128)} %bitcast.21, ...), custom_call_target="tpu_custom_call" | custom-call | tf_op jit(solution)/shard_map/main_step/pallas_call | solution.py:400
  199.9 5.1 %final_step.1 = (bf16[4096,256]{1,0:T(8,128)(2,1)}, f32[256,256]{1,0:T(8,128)}, f32[256,256]{1,0:T(8,128)}) custom-call(bf16[4096,256]{1,0:T(8,128)(2,1)} %get-tuple-element.10.gradh_ref, bf16[4096,256]{1,0:T(8,128)(2,1)} %bitcast.16, bf16[256,256]{1,0:T(8,128)(2,1)} %w_ref.3, f32[256,256]{1,0:T(8,128)} %get-tuple-element.12.msg_ref, ...), custom_call_target="tpu_custom_call" | custom-call | tf_op jit(solution)/shard_map/final_step/pallas_call | solution.py:447

commit v7 on v6

--- a/solution.py
+++ b/solution.py
@@ -20,8 +20,8 @@
     return lax.broadcasted_iota(jnp.int32, shape, dim)
 
 
-def index_tables(slab_ref, local_ref, remote_ref, weight_ref, node_ref, scale_ref, ext_ref):
-    slabs, cap = node_ref.shape[0], node_ref.shape[1]
+def index_tables(slab_ref, local_ref, remote_ref, weight_ref, pair_ref, ext_ref):
+    slabs, cap = ext_ref.shape[0], pair_ref.shape[0]
     chunks = slab_ref.shape[0]
     slab = slab_ref[...]
     ids = iota((chunks, slabs, 128), 1)
@@ -63,11 +63,10 @@
         rows = [part[s : s + 1, q * half : (q + 1) * half] for part in (upper_part, lower_part) for q in range(2)]
         block = jnp.concatenate(rows + [jnp.zeros((EXT - 4, half), F32)], axis=0)
         ext_ref[s] = block.astype(BF16)
-    turned = jnp.transpose(table)
-    for s in range(slabs):
-        at = lambda v: turned[:, v * slabs + s : v * slabs + s + 1]
-        node_ref[s] = jnp.broadcast_to((at(2) * 64.0 + at(3)).astype(jnp.int32), (cap, 128))
-        scale_ref[s] = jnp.broadcast_to(at(4) + at(5) + at(6), (cap, 128))
+    row = lambda v: table[v * slabs : (v + 1) * slabs]
+    node, scale = row(2) * 64.0 + row(3), row(4) + row(5) + row(6)
+    empty = jnp.zeros((128 - 2 * slabs, cap), F32)
+    pair_ref[...] = jnp.transpose(jnp.concatenate([node, scale, empty], axis=0))
 
 
 def sum_scratch(parts, slabs, width):
@@ -177,23 +176,24 @@
     order_ref[...] = jnp.concatenate(rows, axis=0).astype(jnp.int32)
 
 
-FAR = ((2, 1), (1, 1), (3, 1), (0, 1), (2, 0), (1, 0), (3, 0))
+SPLIT = 80
 
 
 def main_kernel(
     parts, slabs, factor,
     picks_ref, slab_ref, local_ref, remote_ref, weight_ref, cols_ref, w_ref, grad_hbm, pre_hbm, feats_hbm, tiles_hbm,
     gradh_hbm, spread_hbm, out_msg_ref, out_upd_ref,
-    node_ref, scale_ref, ext_ref, out_buf, in_buf, grad_ref, pre_ref, acc_ref, gp_ref, stage_ref, got_ref,
+    pair_ref, ext_ref, out_buf, in_buf, grad_ref, pre_ref, acc_ref, gp_ref,
+    near_ref, far_ref, side_ref, stage_a, stage_b, got_ref,
     tiles_ref, run_ref, turned_ref, order_ref, order_smem, msg_ref, upd_ref,
     load_sem, rec_send, rec_recv, blk_send, blk_recv, store_sem, *scratch,
 ):
     b, g = lax.axis_index("blk"), lax.axis_index("grp")
     y, xh = b // 2, b % 2
     xl, z, core = g // 8, (g // 2) % 4, g % 2
-    cap = node_ref.shape[1]
+    cap = pair_ref.shape[0]
     nodes, width = acc_ref.shape
-    picks = stage_ref.shape[1]
+    picks = stage_a.shape[1]
 
     load_grad = pltpu.make_async_copy(grad_hbm, grad_ref, load_sem.at[0])
     load_pre = pltpu.make_async_copy(pre_hbm, pre_ref, load_sem.at[1])
@@ -208,17 +208,16 @@
         dz, dx, dc = (n % 4 + 1) % 4, 1 - n // 8, (q + q // 2) % 2
         return ((xl + dx) % 2 * 4 + (z + dz) % 4) * 2 + (core + dc) % 2
 
-    def blk_peer(n):
-        dy, dx = FAR[n]
-        return (y + dy) % 4 * 2 + (xh + dx) % 2
+    ring = parts // 2
+    up, down, across, side = [(y + dy) % ring * 2 + (xh + dx) % 2 for dy, dx in ((1, 0), (ring - 1, 0), (2, 0), (0, 1))]
 
     barrier = pltpu.get_barrier_semaphore()
     for n in range(slabs - 1):
         pl.semaphore_signal(barrier, inc=1, device_id={"grp": rec_peer(n)}, device_id_type=MESH)
     for n in range(parts - 1):
-        pl.semaphore_signal(barrier, inc=1, device_id={"blk": blk_peer(n)}, device_id_type=MESH)
-
-    index_tables(slab_ref, local_ref, remote_ref, weight_ref, node_ref, scale_ref, ext_ref)
+        pl.semaphore_signal(barrier, inc=1, device_id={"blk": lax.rem(b + n + 1, parts)}, device_id_type=MESH)
+
+    index_tables(slab_ref, local_ref, remote_ref, weight_ref, pair_ref, ext_ref)
     load_grad.wait()
     pl.semaphore_wait(barrier, slabs + parts - 2)
 
@@ -234,7 +233,9 @@
 
     def gather(n, _):
         s = rec_peer(n)
-        node = node_ref[s]
+        lane = iota((cap, 128), 1)
+        column = lambda at: jnp.sum(jnp.where(lane == at, pair_ref[...], 0.0), axis=1, keepdims=True)
+        node = jnp.broadcast_to(column(s).astype(jnp.int32), (cap, 128))
         total = jnp.zeros((cap, width), F32)
         for k in range(nodes // wide):
             pieces = [
@@ -244,8 +245,7 @@
             total += jnp.dot(
                 jnp.concatenate(pieces, axis=1), grad_ref[k * wide : (k + 1) * wide], preferred_element_type=F32
             )
-        scale = scale_ref[s]
-        out_buf[n, :cap] = (total * jnp.concatenate([scale, scale], axis=1)).astype(BF16)
+        out_buf[n, :cap] = (total * column(s + slabs)).astype(BF16)
         out_buf[n, cap:] = ext_ref[s]
 
         @pl.when(n < own)
@@ -300,28 +300,72 @@
         upd_ref[...] += lax.dot_general(act, gradh, TN, preferred_element_type=F32)
         return 0
 
-    lax.fori_loop(0, nodes // 256, finish, 0)
+    copies = {}
+
+    def send(m, src, dst, peer):
+        copies[m] = pltpu.make_async_remote_copy(
+            src, dst, blk_send.at[m], blk_recv.at[m], device_id={"blk": peer}, device_id_type=MESH
+        )
+        copies[m].start()
+
+    panels = nodes // 128
+    low, high = pl.ds(0, panels // 2), pl.ds(panels // 2, panels // 2)
+    rows_a, rows_b = pl.ds(0, SPLIT), pl.ds(SPLIT, 128 - SPLIT)
+    lax.fori_loop(0, nodes // 512, finish, 0)
+    send(0, gp_ref.at[low, rows_a], near_ref.at[0, low], up)
+    lax.fori_loop(nodes // 512, nodes // 256, finish, 0)
+    send(1, gp_ref.at[high, rows_a], near_ref.at[1, high], down)
+    send(4, gp_ref.at[:, rows_b], side_ref, side)
+    send(2, gp_ref.at[high, rows_a], near_ref.at[0, high], up)
+    send(3, gp_ref.at[low, rows_a], near_ref.at[1, low], down)
     load_feats.start()
     store_gradh = pltpu.make_async_copy(grad_ref, gradh_hbm, store_sem.at[0])
     store_gradh.start()
 
-    def pack(to_ref, at, c):
+    def pack(store, load, c, r):
         def one(t, _):
-            to_ref[at + t] = gp_ref[picks_ref[c, b, t]]
+            store(t, load(picks_ref[c, r, t]))
             return 0
 
         lax.fori_loop(0, picks, one, 0)
 
-    sends = []
-    for n in range(parts - 1):
-        pack(stage_ref.at[n], 0, blk_peer(n))
-        copy = pltpu.make_async_remote_copy(
-            stage_ref.at[n], got_ref.at[pl.ds(b * picks, picks)], blk_send.at[n], blk_recv.at[n],
-            device_id={"blk": blk_peer(n)}, device_id_type=MESH,
-        )
-        copy.start()
-        sends.append(copy)
-    pack(got_ref, b * picks, b)
+    def to_stage(ref, n):
+        def store(t, value):
+            ref[n, t] = value
+
+        return store
+
+    def to_got(r, rows):
+        def store(t, value):
+            got_ref[r * picks + t, rows] = value
+
+        return store
+
+    top, rest, whole = slice(0, SPLIT), slice(SPLIT, 128), slice(0, 128)
+    place = lambda r, rows: got_ref.at[pl.ds(r * picks, picks), rows]
+    near = [lambda i: near_ref[0, i], lambda i: near_ref[1, i]]
+    pack(to_stage(stage_a, 0), lambda i: gp_ref[i, top], side, b)
+    send(5, stage_a.at[0], place(b, rows_a), side)
+    copies[0].wait_recv()
+    copies[1].wait_recv()
+    send(6, near_ref.at[0, low], far_ref.at[low], up)
+    send(7, near_ref.at[1, high], far_ref.at[high], down)
+    for n, peer in enumerate((up, down, across)):
+        pack(to_stage(stage_b, n), lambda i: gp_ref[i, rest], peer, b)
+        send(8 + n, stage_b.at[n], place(b, rows_b), peer)
+    copies[2].wait_recv()
+    copies[3].wait_recv()
+    for n, r in enumerate((down, up)):
+        pack(to_stage(stage_a, 1 + n), near[n], side, r)
+        send(11 + n, stage_a.at[1 + n], place(r, rows_a), side)
+    copies[4].wait_recv()
+    for n, peer in enumerate((up, down, across)):
+        pack(to_stage(stage_b, 3 + n), lambda i: side_ref[i], peer, side)
+        send(13 + n, stage_b.at[3 + n], place(side, rows_b), peer)
+    pack(to_got(b, whole), lambda i: gp_ref[i], b, b)
+    pack(to_got(down, top), near[0], b, down)
+    pack(to_got(up, top), near[1], b, up)
+    pack(to_got(side, rest), lambda i: side_ref[i], b, side)
 
     column_order(cols_ref, order_ref)
     to_smem = pltpu.make_async_copy(order_ref, order_smem, store_sem.at[1])
@@ -334,6 +378,11 @@
         return 0
 
     lax.fori_loop(0, tiles, turn, 0)
+    copies[6].wait_recv()
+    copies[7].wait_recv()
+    pack(to_stage(stage_a, 3), lambda i: far_ref[i], side, across)
+    send(16, stage_a.at[3], place(across, rows_a), side)
+    pack(to_got(across, top), lambda i: far_ref[i], b, across)
     load_feats.wait()
 
     def turn_feats(k, _):
@@ -345,8 +394,10 @@
     to_smem.wait()
     lax.fori_loop(0, slabs - 1, lambda n, x: (rec_copy(n).wait_send(), x)[1], 0)
     store_gradh.wait()
-    for copy in sends:
-        copy.wait()
+    for m in (5, 8, 9, 10, 11, 12, 13, 14, 15, 16):
+        copies[m].wait_recv()
+    for m in range(len(copies)):
+        copies[m].wait_send()
 
     half = len(scratch) // 2
     upd_sum = sum_stages(parts, slabs, factor, upd_ref, out_upd_ref, scratch[:half])
@@ -403,8 +454,7 @@
         in_specs=[pl.BlockSpec(memory_space=pltpu.SMEM)] + [vmem] * 6 + [hbm] * 4,
         out_specs=[hbm, hbm, vmem, vmem],
         scratch_shapes=[
-            pltpu.VMEM((slabs, cap, 128), jnp.int32),
-            pltpu.VMEM((slabs, cap, 128), F32),
+            pltpu.VMEM((cap, 128), F32),
             pltpu.VMEM((slabs, EXT, width), BF16),
             pltpu.VMEM((slabs, cap + EXT, width), BF16),
             pltpu.VMEM((slabs, cap + EXT, width), BF16),
@@ -412,7 +462,11 @@
             pltpu.VMEM((nodes, width), BF16),
             pltpu.VMEM((nodes, width), F32),
             pltpu.VMEM((nodes // 128, 128, width), BF16),
-            pltpu.VMEM((parts - 1, count, 128, width), BF16),
+            pltpu.VMEM((2, nodes // 128, SPLIT, width), BF16),
+            pltpu.VMEM((nodes // 128, SPLIT, width), BF16),
+            pltpu.VMEM((nodes // 128, 128 - SPLIT, width), BF16),
+            pltpu.VMEM((4, count, SPLIT, width), BF16),
+            pltpu.VMEM((6, count, 128 - SPLIT, width), BF16),
             pltpu.VMEM((parts * count, 128, width), BF16),
             pltpu.VMEM((parts * count, 128, 128), BF16),
             pltpu.VMEM((parts * count, 128, width), BF16),
@@ -421,7 +475,7 @@
             pltpu.SMEM((8, parts * count), jnp.int32),
             pltpu.VMEM((width, width), F32),
             pltpu.VMEM((width, width), F32),
-            dma((4,)), dma((slabs - 1,)), dma((slabs,)), dma((parts - 1,)), dma((parts - 1,)), dma((3,)),
+            dma((4,)), dma((slabs - 1,)), dma((slabs,)), dma((17,)), dma((17,)), dma((3,)),
         ]
         + sum_scratch(parts, slabs, width) * 2,
         compiler_params=pltpu.CompilerParams(collective_id=0, has_side_effects=True, vmem_limit_bytes=VMEM_LIMIT),

time: 205 us -> 189 us (0.922)
  Pallas kernels: 204 us -> 188 us
    pallas_call x1, Pallas kernels: 199 us -> 183 us  [main_step(): pl.pallas_call(functools.partial(main_kernel, parts, slabs, factor), out_...]
where the time goes in v7:
time: 189 us; the launch traced here: 188 us
  Pallas kernels  188 us (99%)
    pallas_call x1, Pallas kernels, main_step(): pl.pallas_call(functools.partial(main_kernel, parts, slabs, factor), out_...  183 us
    pallas_call x1, Pallas kernels, final_step(): pl.pallas_call(final_kernel, grid=(rows // tall,), out_shape=[jax.ShapeDt...  5.12 us

profile of v7, /device:TPU:1, one launch (start us, length us, event | category | flops | bytes accessed | tf_op | source)
XLA Modules:
  0.0 188.4 jit_solution(6626835320840605063)
XLA Ops:
  0.6 182.6 %main_step.1 = (bf16[4096,256]{1,0:T(8,128)(2,1)}, bf16[32,128,256]{2,1,0:T(8,128)(2,1)}, f32[256,256]{1,0:T(8,128)}, f32[256,256]{1,0:T(8,128)}) custom-call(s32[8,8,16]{2,1,0:T(8,128)} %bitcast.17, s32[32,128]{1,0:T(8,128)} %bitcast.18, s32[32,128]{1,0:T(8,128)} %bitcast.19, s32[32,128]{1,0:T(8,128)} %bitcast.20, f32[32,128]{1,0:T(8,128)} %bitcast.21, ...), custom_call_target="tpu_custom_call" | custom-call | tf_op jit(solution)/shard_map/main_step/pallas_call | solution.py:451
  183.2 5.1 %final_step.1 = (bf16[4096,256]{1,0:T(8,128)(2,1)}, f32[256,256]{1,0:T(8,128)}, f32[256,256]{1,0:T(8,128)}) custom-call(bf16[4096,256]{1,0:T(8,128)(2,1)} %get-tuple-element.10.gradh_ref, bf16[4096,256]{1,0:T(8,128)(2,1)} %bitcast.16, bf16[256,256]{1,0:T(8,128)(2,1)} %w_ref.3, f32[256,256]{1,0:T(8,128)} %get-tuple-element.12.msg_ref, ...), custom_call_target="tpu_custom_call" | custom-call | tf_op jit(solution)/shard_map/final_step/pallas_call | solution.py:501

commit v8 on v7

--- a/solution.py
+++ b/solution.py
@@ -153,13 +153,14 @@
     return split_blk, split_grp, join_grp, join_blk, finish
 
 
-def column_order(cols_ref, order_ref):
-    parts, picks = cols_ref.shape
+def column_order(cols, early, order_ref):
+    parts, picks = cols.shape
     count = parts * picks
     repeat = jnp.where(iota((picks, count), 1) % picks == iota((picks, count), 0), 1.0, 0.0).astype(BF16)
-    wide = jnp.dot(cols_ref[...].astype(F32).astype(BF16), repeat, preferred_element_type=F32)
+    wide = jnp.dot(cols.astype(F32).astype(BF16), repeat, preferred_element_type=F32)
     own = jnp.where(iota((parts, count), 1) // picks == iota((parts, count), 0), wide, 0.0)
-    cols = jnp.broadcast_to(jnp.sum(own, axis=0, keepdims=True), (count, count))
+    line = jnp.sum(own, axis=0, keepdims=True) + jnp.where(iota((1, count), 1) >= early, 32.0, 0.0)
+    cols = jnp.broadcast_to(line, (count, count))
     across, down = iota((count, count), 1).astype(F32), iota((count, count), 0).astype(F32)
     turned = jnp.transpose(cols)
     ones = lambda hit: jnp.where(hit, 1.0, 0.0)
@@ -181,12 +182,12 @@
 
 def main_kernel(
     parts, slabs, factor,
-    picks_ref, slab_ref, local_ref, remote_ref, weight_ref, cols_ref, w_ref, grad_hbm, pre_hbm, feats_hbm, tiles_hbm,
-    gradh_hbm, spread_hbm, out_msg_ref, out_upd_ref,
-    pair_ref, ext_ref, out_buf, in_buf, grad_ref, pre_ref, acc_ref, gp_ref,
-    near_ref, far_ref, side_ref, stage_a, stage_b, got_ref,
+    picks_ref, slab_ref, local_ref, remote_ref, weight_ref, cols_ref, w_ref, wm_ref, grad_hbm, pre_hbm, feats_hbm, tiles_hbm,
+    out_hbm, out_msg_ref, out_upd_ref,
+    pair_ref, ext_ref, out_buf, in_buf, grad_ref, pre_ref, acc_ref, slope_ref, gp_ref,
+    near_ref, far_ref, side_ref, stage_a, stage_b, early_ref, late_ref,
     tiles_ref, run_ref, turned_ref, order_ref, order_smem, msg_ref, upd_ref,
-    load_sem, rec_send, rec_recv, blk_send, blk_recv, store_sem, *scratch,
+    load_sem, tile_sem, rec_send, rec_recv, blk_send, blk_recv, store_sem, *scratch,
 ):
     b, g = lax.axis_index("blk"), lax.axis_index("grp")
     y, xh = b // 2, b % 2
@@ -197,11 +198,9 @@
 
     load_grad = pltpu.make_async_copy(grad_hbm, grad_ref, load_sem.at[0])
     load_pre = pltpu.make_async_copy(pre_hbm, pre_ref, load_sem.at[1])
-    load_tiles = pltpu.make_async_copy(tiles_hbm, tiles_ref, load_sem.at[2])
-    load_feats = pltpu.make_async_copy(feats_hbm, pre_ref, load_sem.at[3])
+    load_feats = pltpu.make_async_copy(feats_hbm, pre_ref, load_sem.at[2])
     load_grad.start()
     load_pre.start()
-    load_tiles.start()
 
     def rec_peer(n):
         q = n // 4
@@ -209,7 +208,17 @@
         return ((xl + dx) % 2 * 4 + (z + dz) % 4) * 2 + (core + dc) % 2
 
     ring = parts // 2
-    up, down, across, side = [(y + dy) % ring * 2 + (xh + dx) % 2 for dy, dx in ((1, 0), (ring - 1, 0), (2, 0), (0, 1))]
+    spot = lambda dy, dx: (y + dy) % ring * 2 + (xh + dx) % 2
+    up, down, across, side = spot(1, 0), spot(ring - 1, 0), spot(2, 0), spot(0, 1)
+    owners = (b, down, up, side, across, spot(ring - 1, 1), spot(1, 1), spot(2, 1))
+    load_tiles = [
+        pltpu.make_async_copy(
+            tiles_hbm.at[pl.ds(r * picks, picks)], tiles_ref.at[pl.ds(k * picks, picks)], tile_sem.at[k]
+        )
+        for k, r in enumerate(owners)
+    ]
+    for load in load_tiles:
+        load.start()
 
     barrier = pltpu.get_barrier_semaphore()
     for n in range(slabs - 1):
@@ -257,6 +266,18 @@
     lax.fori_loop(0, slabs, gather, 0)
     own_copy.start()
     acc_ref[...] = grad_ref[...].astype(F32)
+    load_pre.wait()
+
+    def slopes(i, _):
+        at = pl.ds(pl.multiple_of(i * 256, 256), 256)
+        pre = pre_ref[at].astype(F32)
+        sig = 1.0 / (1.0 + jnp.exp(-pre))
+        slope_ref[at] = sig * (1.0 + pre * (1.0 - sig))
+        turned_ref[i] = jnp.transpose((pre * sig).astype(BF16))
+        return 0
+
+    lax.fori_loop(0, nodes // 256, slopes, 0)
+    load_feats.start()
     own_copy.wait()
 
     tall = 1024
@@ -284,20 +305,12 @@
 
     lax.fori_loop(0, slabs, scatter, 0)
 
-    load_pre.wait()
-    upd_ref[...] = jnp.zeros_like(upd_ref)
-
     def finish(i, _):
-        at = pl.ds(pl.multiple_of(i * 256, 256), 256)
+        at = pl.ds(pl.multiple_of(i * 512, 512), 512)
         gradh = acc_ref[at].astype(BF16)
         grad_ref[at] = gradh
-        pre = pre_ref[at].astype(F32)
-        sig = 1.0 / (1.0 + jnp.exp(-pre))
-        act = (pre * sig).astype(BF16)
-        slope = sig * (1.0 + pre * (1.0 - sig))
         back = lax.dot_general(gradh, w_ref[...], NT, preferred_element_type=F32)
-        gp_ref[pl.ds(i * 2, 2)] = (back * slope).astype(BF16).reshape(2, 128, width)
-        upd_ref[...] += lax.dot_general(act, gradh, TN, preferred_element_type=F32)
+        gp_ref[pl.ds(i * 4, 4)] = (back * slope_ref[at]).astype(BF16).reshape(4, 128, width)
         return 0
 
     copies = {}
@@ -311,17 +324,13 @@
     panels = nodes // 128
     low, high = pl.ds(0, panels // 2), pl.ds(panels // 2, panels // 2)
     rows_a, rows_b = pl.ds(0, SPLIT), pl.ds(SPLIT, 128 - SPLIT)
-    lax.fori_loop(0, nodes // 512, finish, 0)
+    lax.fori_loop(0, nodes // 1024, finish, 0)
     send(0, gp_ref.at[low, rows_a], near_ref.at[0, low], up)
-    lax.fori_loop(nodes // 512, nodes // 256, finish, 0)
+    lax.fori_loop(nodes // 1024, nodes // 512, finish, 0)
     send(1, gp_ref.at[high, rows_a], near_ref.at[1, high], down)
     send(4, gp_ref.at[:, rows_b], side_ref, side)
     send(2, gp_ref.at[high, rows_a], near_ref.at[0, high], up)
     send(3, gp_ref.at[low, rows_a], near_ref.at[1, low], down)
-    load_feats.start()
-    store_gradh = pltpu.make_async_copy(grad_ref, gradh_hbm, store_sem.at[0])
-    store_gradh.start()
-
     def pack(store, load, c, r):
         def one(t, _):
             store(t, load(picks_ref[c, r, t]))
@@ -335,42 +344,45 @@
 
         return store
 
-    def to_got(r, rows):
+    def to_early(slot, rows):
         def store(t, value):
-            got_ref[r * picks + t, rows] = value
+            early_ref[slot * picks + t, rows] = value
 
         return store
 
     top, rest, whole = slice(0, SPLIT), slice(SPLIT, 128), slice(0, 128)
-    place = lambda r, rows: got_ref.at[pl.ds(r * picks, picks), rows]
+    place = lambda ref, slot, rows: ref.at[pl.ds(slot * picks, picks), rows]
     near = [lambda i: near_ref[0, i], lambda i: near_ref[1, i]]
     pack(to_stage(stage_a, 0), lambda i: gp_ref[i, top], side, b)
-    send(5, stage_a.at[0], place(b, rows_a), side)
+    send(5, stage_a.at[0], place(early_ref, 3, rows_a), side)
     copies[0].wait_recv()
     copies[1].wait_recv()
     send(6, near_ref.at[0, low], far_ref.at[low], up)
     send(7, near_ref.at[1, high], far_ref.at[high], down)
     for n, peer in enumerate((up, down, across)):
         pack(to_stage(stage_b, n), lambda i: gp_ref[i, rest], peer, b)
-        send(8 + n, stage_b.at[n], place(b, rows_b), peer)
+        send(8 + n, stage_b.at[n], place(early_ref, (1, 2, 4)[n], rows_b), peer)
     copies[2].wait_recv()
     copies[3].wait_recv()
     for n, r in enumerate((down, up)):
         pack(to_stage(stage_a, 1 + n), near[n], side, r)
-        send(11 + n, stage_a.at[1 + n], place(r, rows_a), side)
+        send(11 + n, stage_a.at[1 + n], place(late_ref, n, rows_a), side)
     copies[4].wait_recv()
     for n, peer in enumerate((up, down, across)):
         pack(to_stage(stage_b, 3 + n), lambda i: side_ref[i], peer, side)
-        send(13 + n, stage_b.at[3 + n], place(side, rows_b), peer)
-    pack(to_got(b, whole), lambda i: gp_ref[i], b, b)
-    pack(to_got(down, top), near[0], b, down)
-    pack(to_got(up, top), near[1], b, up)
-    pack(to_got(side, rest), lambda i: side_ref[i], b, side)
-
-    column_order(cols_ref, order_ref)
-    to_smem = pltpu.make_async_copy(order_ref, order_smem, store_sem.at[1])
+        send(13 + n, stage_b.at[3 + n], place(late_ref, n, rows_b), peer)
+    pack(to_early(0, whole), lambda i: gp_ref[i], b, b)
+    pack(to_early(1, top), near[0], b, down)
+    pack(to_early(2, top), near[1], b, up)
+    pack(to_early(3, rest), lambda i: side_ref[i], b, side)
+
+    cols = jnp.concatenate([cols_ref[pl.ds(r, 1)] for r in owners], axis=0)
+    early = 5 * picks
+    column_order(cols, early, order_ref)
+    to_smem = pltpu.make_async_copy(order_ref, order_smem, store_sem.at[0])
     to_smem.start()
-    load_tiles.wait()
+    for load in load_tiles:
+        load.wait()
     tiles = parts * picks
 
     def turn(k, _):
@@ -381,8 +393,17 @@
     copies[6].wait_recv()
     copies[7].wait_recv()
     pack(to_stage(stage_a, 3), lambda i: far_ref[i], side, across)
-    send(16, stage_a.at[3], place(across, rows_a), side)
-    pack(to_got(across, top), lambda i: far_ref[i], b, across)
+    send(16, stage_a.at[3], place(late_ref, 2, rows_a), side)
+    pack(to_early(4, top), lambda i: far_ref[i], b, across)
+
+    upd_ref[...] = jnp.zeros_like(upd_ref)
+
+    def update(i, _):
+        at = pl.ds(pl.multiple_of(i * 256, 256), 256)
+        upd_ref[...] += jnp.dot(turned_ref[i], grad_ref[at], preferred_element_type=F32)
+        return 0
+
+    lax.fori_loop(0, nodes // 256, update, 0)
     load_feats.wait()
 
     def turn_feats(k, _):
@@ -393,37 +414,39 @@
     lax.fori_loop(0, nodes // 256, turn_feats, 0)
     to_smem.wait()
     lax.fori_loop(0, slabs - 1, lambda n, x: (rec_copy(n).wait_send(), x)[1], 0)
-    store_gradh.wait()
-    for m in (5, 8, 9, 10, 11, 12, 13, 14, 15, 16):
+    group = 8
+
+    def products(ref, start, size):
+        def step(m, total):
+            for q in range(group):
+                k = m * group + q
+                f = lax.clamp(start, order_smem[0, k], start + size - 1)
+                part = jnp.dot(tiles_ref[f], ref[f - start], preferred_element_type=F32)
+                total = total * order_smem[1, k].astype(F32) + part
+                run_ref[k] = total.astype(BF16)
+            return total
+
+        lax.fori_loop(start // group, (start + size) // group, step, jnp.zeros((128, width), F32))
+
+    for m in (5, 8, 9, 10):
         copies[m].wait_recv()
-    for m in range(len(copies)):
-        copies[m].wait_send()
-
+    products(early_ref, 0, early)
+    for m in (11, 12, 13, 14, 15, 16):
+        copies[m].wait_recv()
     half = len(scratch) // 2
     upd_sum = sum_stages(parts, slabs, factor, upd_ref, out_upd_ref, scratch[:half])
     msg_sum = sum_stages(parts, slabs, factor, msg_ref, out_msg_ref, scratch[half:])
     upd_sum[0]()
-    group = 8
-
-    def products(m, total):
-        for q in range(group):
-            k = m * group + q
-            f = lax.clamp(0, order_smem[0, k], tiles - 1)
-            part = jnp.dot(tiles_ref[f], got_ref[f], preferred_element_type=F32)
-            total = total * order_smem[1, k].astype(F32) + part
-            run_ref[k] = total.astype(BF16)
-        return total
-
-    lax.fori_loop(0, tiles // group, products, jnp.zeros((128, width), F32))
+    products(late_ref, early, tiles - early)
+    for m in range(len(copies)):
+        copies[m].wait_send()
 
     def settle(j, _):
-        last = run_ref[lax.clamp(0, order_smem[2, j], tiles - 1)]
-        gp_ref[j] = (last.astype(F32) * order_smem[3, j].astype(F32)).astype(BF16)
-        return 0
-
-    lax.fori_loop(0, nodes // 128, settle, 0)
-    store_spread = pltpu.make_async_copy(gp_ref, spread_hbm, store_sem.at[2])
-    store_spread.start()
+        piece = lambda k: run_ref[lax.clamp(0, order_smem[2, k], tiles - 1)].astype(F32) * order_smem[3, k].astype(F32)
+        gp_ref[j] = (piece(j) + piece(j + panels)).astype(BF16)
+        return 0
+
+    lax.fori_loop(0, panels, settle, 0)
     upd_sum[1]()
     msg = jnp.zeros((width, width), F32)
     for k in range(nodes // 256):
@@ -431,28 +454,41 @@
     msg_ref[...] = msg
     msg_sum[0]()
     upd_sum[2]()
+
+    def features(i, _):
+        at = pl.ds(pl.multiple_of(i * 512, 512), 512)
+        spread = gp_ref[pl.ds(i * 4, 4)].reshape(512, width)
+        below = lax.dot_general(spread, wm_ref[...], NT, preferred_element_type=F32)
+        pre_ref[at] = (grad_ref[at].astype(F32) + below).astype(BF16)
+        return 0
+
+    lax.fori_loop(0, nodes // 512, features, 0)
+    store_out = pltpu.make_async_copy(pre_ref, out_hbm, store_sem.at[1])
+    store_out.start()
     msg_sum[1]()
     upd_sum[3]()
     msg_sum[2]()
     msg_sum[3]()
     upd_sum[4]()
     msg_sum[4]()
-    store_spread.wait()
-
-
-def main_step(picks, slab, local, remote, weight, cols, w_update, grad, pre, feats, tiles, slabs, parts, cap, factor):
+    store_out.wait()
+
+
+def main_step(
+    picks, slab, local, remote, weight, cols, w_update, w_message, grad, pre, feats, tiles, slabs, parts, cap, factor
+):
     nodes, width = grad.shape
     count = picks.shape[-1]
+    panels, early = nodes // 128, 5 * count
     vmem = pl.BlockSpec(memory_space=pltpu.VMEM)
     hbm = pl.BlockSpec(memory_space=pl.ANY)
     dma = pltpu.SemaphoreType.DMA
-    panels = jax.ShapeDtypeStruct((nodes // 128, 128, width), BF16)
     square = jax.ShapeDtypeStruct((width, width), F32)
     return pl.pallas_call(
         functools.partial(main_kernel, parts, slabs, factor),
-        out_shape=[jax.ShapeDtypeStruct((nodes, width), BF16), panels, square, square],
-        in_specs=[pl.BlockSpec(memory_space=pltpu.SMEM)] + [vmem] * 6 + [hbm] * 4,
-        out_specs=[hbm, hbm, vmem, vmem],
+        out_shape=[jax.ShapeDtypeStruct((nodes, width), BF16), square, square],
+        in_specs=[pl.BlockSpec(memory_space=pltpu.SMEM)] + [vmem] * 7 + [hbm] * 4,
+        out_specs=[hbm, vmem, vmem],
         scratch_shapes=[
             pltpu.VMEM((cap, 128), F32),
             pltpu.VMEM((slabs, EXT, width), BF16),
@@ -461,13 +497,15 @@
             pltpu.VMEM((nodes, width), BF16),
             pltpu.VMEM((nodes, width), BF16),
             pltpu.VMEM((nodes, width), F32),
-            pltpu.VMEM((nodes // 128, 128, width), BF16),
-            pltpu.VMEM((2, nodes // 128, SPLIT, width), BF16),
-            pltpu.VMEM((nodes // 128, SPLIT, width), BF16),
-            pltpu.VMEM((nodes // 128, 128 - SPLIT, width), BF16),
+            pltpu.VMEM((nodes, width), F32),
+            pltpu.VMEM((panels, 128, width), BF16),
+            pltpu.VMEM((2, panels, SPLIT, width), BF16),
+            pltpu.VMEM((panels, SPLIT, width), BF16),
+            pltpu.VMEM((panels, 128 - SPLIT, width), BF16),
             pltpu.VMEM((4, count, SPLIT, width), BF16),
             pltpu.VMEM((6, count, 128 - SPLIT, width), BF16),
-            pltpu.VMEM((parts * count, 128, width), BF16),
+            pltpu.VMEM((early, 128, width), BF16),
+            pltpu.VMEM((parts * count - early, 128, width), BF16),
             pltpu.VMEM((parts * count, 128, 128), BF16),
             pltpu.VMEM((parts * count, 128, width), BF16),
             pltpu.VMEM((nodes // 256, width, 256), BF16),
@@ -475,38 +513,37 @@
             pltpu.SMEM((8, parts * count), jnp.int32),
             pltpu.VMEM((width, width), F32),
             pltpu.VMEM((width, width), F32),
-            dma((4,)), dma((slabs - 1,)), dma((slabs,)), dma((17,)), dma((17,)), dma((3,)),
+            dma((3,)), dma((parts,)), dma((slabs - 1,)), dma((slabs,)), dma((17,)), dma((17,)), dma((2,)),
         ]
         + sum_scratch(parts, slabs, width) * 2,
         compiler_params=pltpu.CompilerParams(collective_id=0, has_side_effects=True, vmem_limit_bytes=VMEM_LIMIT),
         name="main_step",
-    )(picks, slab, local, remote, weight, cols, w_update, grad, pre, feats, tiles)
-
-
-def final_kernel(gradh_ref, spread_ref, w_ref, msg_ref, upd_ref, out_ref, out_msg_ref, out_upd_ref):
-    down = lax.dot_general(spread_ref[...], w_ref[...], NT, preferred_element_type=F32)
-    out_ref[...] = (gradh_ref[...].astype(F32) + down).astype(BF16)
-
-    @pl.when(pl.program_id(0) == 0)
-    def _():
-        out_msg_ref[...] = msg_ref[...]
-        out_upd_ref[...] = upd_ref[...]
-
-
-def final_step(gradh, spread, w_message, msg, upd):
-    rows, width = gradh.shape
-    tall = rows // 4
-    tile = pl.BlockSpec((tall, width), lambda i: (i, 0))
-    square = pl.BlockSpec((width, width), lambda i: (0, 0))
+    )(picks, slab, local, remote, weight, cols, w_update, w_message, grad, pre, feats, tiles)
+
+
+def final_kernel(out_ref, msg_ref, upd_ref, to_out_ref, to_msg_ref, to_upd_ref, sem):
+    rows = out_ref.shape[0] // 4
+    pairs = [(out_ref.at[pl.ds(k * rows, rows)], to_out_ref.at[pl.ds(k * rows, rows)]) for k in range(4)]
+    pairs += [(msg_ref, to_msg_ref), (upd_ref, to_upd_ref)]
+    moves = [pltpu.make_async_copy(src, dst, sem.at[k]) for k, (src, dst) in enumerate(pairs)]
+    for move in moves:
+        move.start()
+    for move in moves:
+        move.wait()
+
+
+def final_step(out, msg, upd):
+    hbm = pl.BlockSpec(memory_space=pl.ANY)
+    args = (out, msg, upd)
     return pl.pallas_call(
         final_kernel,
-        grid=(rows // tall,),
-        out_shape=[jax.ShapeDtypeStruct(gradh.shape, BF16)] + [jax.ShapeDtypeStruct(msg.shape, F32)] * 2,
-        in_specs=[tile, tile, square, square, square],
-        out_specs=[tile, square, square],
+        out_shape=[jax.ShapeDtypeStruct(a.shape, a.dtype) for a in args],
+        in_specs=[hbm] * 3,
+        out_specs=[hbm] * 3,
+        scratch_shapes=[pltpu.SemaphoreType.DMA((6,))],
         compiler_params=pltpu.CompilerParams(vmem_limit_bytes=VMEM_LIMIT),
         name="final_step",
-    )(gradh, spread, w_message, msg, upd)
+    )(*args)
 
 
 def local(
@@ -523,12 +560,12 @@
     lanes = lambda a: a.reshape(records // 128, 128)
     tiles = tile_vals[0, 0]
     count = tiles.shape[0] * tiles.shape[1]
-    gradh, spread, msg, upd = main_step(
+    out, msg, upd = main_step(
         tile_rows[0], lanes(rec_slab), lanes(rec_local), lanes(rec_remote), lanes(rec_weight),
-        tile_cols[0, 0], w_update, grad, pre_act[0], node_feats[0],
+        tile_cols[0, 0], w_update, w_message, grad, pre_act[0], node_feats[0],
         tiles.reshape(count, *tiles.shape[2:]), slabs, parts, cap, factor,
     )
-    feats, msg, upd = final_step(gradh, spread.reshape(rows, width), w_message, msg, upd)
+    feats, msg, upd = final_step(out, msg, upd)
     return (feats[None], msg, upd)
 
 

time: 189 us -> 261 us (1.38)
  Pallas kernels: 188 us -> 260 us
    pallas_call x1, Pallas kernels: 5.12 us -> 80.6 us  [final_step(): pl.pallas_call(final_kernel, out_shape=[jax.ShapeDtypeStruct(a.shape, a.d...]
    pallas_call x1, Pallas kernels: 183 us -> 180 us  [main_step(): pl.pallas_call(functools.partial(main_kernel, parts, slabs, factor), out_...]
where the time goes in v8:
time: 261 us
  Pallas kernels  260 us (100%)
    pallas_call x1, Pallas kernels, main_step(): pl.pallas_call(functools.partial(main_kernel, parts, slabs, factor), out_...  180 us
    pallas_call x1, Pallas kernels, final_step(): pl.pallas_call(final_kernel, out_shape=[jax.ShapeDtypeStruct(a.shape, a.d...  80.6 us

profile of v8, /device:TPU:1, one launch (start us, length us, event | category | flops | bytes accessed | tf_op | source)
XLA Modules:
  0.0 261.0 jit_solution(8499777501938423466)
XLA Ops:
  0.6 179.8 %main_step.1 = (bf16[4096,256]{1,0:T(8,128)(2,1)}, f32[256,256]{1,0:T(8,128)}, f32[256,256]{1,0:T(8,128)}) custom-call(s32[8,8,16]{2,1,0:T(8,128)} %bitcast.15, s32[32,128]{1,0:T(8,128)} %bitcast.16, s32[32,128]{1,0:T(8,128)} %bitcast.17, s32[32,128]{1,0:T(8,128)} %bitcast.18, f32[32,128]{1,0:T(8,128)} %bitcast.19, s32[8,16]{1,0:T(8,128)} %bitcast.20, ...), custom_call_target="tpu_custom_call" | custom-call | tf_op jit(solution)/shard_map/main_step/pallas_call | solution.py:487
  180.4 80.6 %final_step.1 = (bf16[4096,256]{1,0:T(8,128)(2,1)}, f32[256,256]{1,0:T(8,128)}, f32[256,256]{1,0:T(8,128)}) custom-call(bf16[4096,256]{1,0:T(8,128)(2,1)} %get-tuple-element.9.out_ref, f32[256,256]{1,0:T(8,128)} %get-tuple-element.10.msg_ref, f32[256,256]{1,0:T(8,128)} %get-tuple-element.11.upd_ref), custom_call_target="tpu_custom_call" | custom-call | tf_op jit(solution)/shard_map/final_step/pallas_call | solution.py:538

commit v9 on v8

--- a/solution.py
+++ b/solution.py
@@ -521,26 +521,22 @@
     )(picks, slab, local, remote, weight, cols, w_update, w_message, grad, pre, feats, tiles)
 
 
-def final_kernel(out_ref, msg_ref, upd_ref, to_out_ref, to_msg_ref, to_upd_ref, sem):
-    rows = out_ref.shape[0] // 4
-    pairs = [(out_ref.at[pl.ds(k * rows, rows)], to_out_ref.at[pl.ds(k * rows, rows)]) for k in range(4)]
-    pairs += [(msg_ref, to_msg_ref), (upd_ref, to_upd_ref)]
-    moves = [pltpu.make_async_copy(src, dst, sem.at[k]) for k, (src, dst) in enumerate(pairs)]
-    for move in moves:
-        move.start()
-    for move in moves:
-        move.wait()
+def final_kernel(out_ref, msg_ref, upd_ref, to_out_ref, to_msg_ref, to_upd_ref):
+    to_out_ref[...] = out_ref[...]
+    to_msg_ref[...] = msg_ref[...]
+    to_upd_ref[...] = upd_ref[...]
 
 
 def final_step(out, msg, upd):
-    hbm = pl.BlockSpec(memory_space=pl.ANY)
+    steps = 4
     args = (out, msg, upd)
+    specs = [pl.BlockSpec((a.shape[0] // steps, a.shape[1]), lambda i: (i, 0)) for a in args]
     return pl.pallas_call(
         final_kernel,
+        grid=(steps,),
         out_shape=[jax.ShapeDtypeStruct(a.shape, a.dtype) for a in args],
-        in_specs=[hbm] * 3,
-        out_specs=[hbm] * 3,
-        scratch_shapes=[pltpu.SemaphoreType.DMA((6,))],
+        in_specs=specs,
+        out_specs=specs,
         compiler_params=pltpu.CompilerParams(vmem_limit_bytes=VMEM_LIMIT),
         name="final_step",
     )(*args)

time: 261 us -> 185 us (0.71)
  Pallas kernels: 260 us -> 184 us
    pallas_call x1, Pallas kernels: 80.6 us -> 3.94 us  [final_step(): pl.pallas_call(final_kernel, grid=(steps,), out_shape=[jax.ShapeDtypeStru...]
where the time goes in v9:
time: 185 us; the launch traced here: 184 us
  Pallas kernels  184 us (99%)
    pallas_call x1, Pallas kernels, main_step(): pl.pallas_call(functools.partial(main_kernel, parts, slabs, factor), out_...  180 us
    pallas_call x1, Pallas kernels, final_step(): pl.pallas_call(final_kernel, grid=(steps,), out_shape=[jax.ShapeDtypeStru...  3.94 us

profile of v9, /device:TPU:1, one launch (start us, length us, event | category | flops | bytes accessed | tf_op | source)
XLA Modules:
  0.0 184.3 jit_solution(2766146523309674639)
XLA Ops:
  0.6 179.8 %main_step.1 = (bf16[4096,256]{1,0:T(8,128)(2,1)}, f32[256,256]{1,0:T(8,128)}, f32[256,256]{1,0:T(8,128)}) custom-call(s32[8,8,16]{2,1,0:T(8,128)} %bitcast.15, s32[32,128]{1,0:T(8,128)} %bitcast.16, s32[32,128]{1,0:T(8,128)} %bitcast.17, s32[32,128]{1,0:T(8,128)} %bitcast.18, f32[32,128]{1,0:T(8,128)} %bitcast.19, s32[8,16]{1,0:T(8,128)} %bitcast.20, ...), custom_call_target="tpu_custom_call" | custom-call | tf_op jit(solution)/shard_map/main_step/pallas_call | solution.py:487
  180.4 3.9 %final_step.1 = (bf16[4096,256]{1,0:T(8,128)(2,1)}, f32[256,256]{1,0:T(8,128)}, f32[256,256]{1,0:T(8,128)}) custom-call(bf16[4096,256]{1,0:T(8,128)(2,1)} %get-tuple-element.9.out_ref, f32[256,256]{1,0:T(8,128)} %get-tuple-element.10.msg_ref, f32[256,256]{1,0:T(8,128)} %get-tuple-element.11.upd_ref), custom_call_target="tpu_custom_call" | custom-call | tf_op jit(solution)/shard_map/final_step/pallas_call | solution.py:534

commit v10 on v9

--- a/solution.py
+++ b/solution.py
@@ -153,6 +153,79 @@
     return split_blk, split_grp, join_grp, join_blk, finish
 
 
+def chip_scratch(parts, slabs):
+    chips = parts * slabs // 2
+    dma = pltpu.SemaphoreType.DMA
+    return [
+        pltpu.VMEM((chips, 8, 128), F32),
+        pltpu.VMEM((chips - 1, 8, 128), F32),
+        pltpu.VMEM((8, 128), F32),
+        pltpu.VMEM((8, 128), F32),
+        pltpu.VMEM((8, 128), F32),
+        pltpu.VMEM((chips, 8, 128), F32),
+        dma, dma, dma, dma, dma, dma,
+    ]
+
+
+def chip_peer(parts, slabs, k):
+    b, g = lax.axis_index("blk"), lax.axis_index("grp")
+    half = slabs // 2
+    return (b + k // half) % parts, (g // 2 + k % half) % half, g % 2
+
+
+def chip_stages(parts, slabs, factor, term_ref, out_ref, scratch):
+    mine, come, part, pair, piece, whole, s1, r1, s2, r2, s3, r3 = scratch
+    b, g = lax.axis_index("blk"), lax.axis_index("grp")
+    half = slabs // 2
+    chips = parts * half
+    me = b * half + g // 2
+    spots = [(slice(c // 2 * 8, c // 2 * 8 + 8), slice(c % 2 * 128, c % 2 * 128 + 128)) for c in range(chips)]
+    many = pl.ds(0, chips - 1)
+    other = pltpu.make_async_remote_copy(
+        part, pair, s2, r2, device_id={"grp": g // 2 * 2 + 1 - g % 2}, device_id_type=MESH
+    )
+
+    def spread(src, dst, send, recv):
+        def one(k, _):
+            pb, pq, core = chip_peer(parts, slabs, k)
+            pltpu.make_async_remote_copy(
+                src(pb * half + pq), dst(k), send, recv,
+                device_id={"blk": pb, "grp": pq * 2 + core}, device_id_type=MESH,
+            ).start()
+            return 0
+
+        lax.fori_loop(1, chips, one, 0)
+
+    def split():
+        for c in range(chips):
+            mine[c] = term_ref[spots[c]]
+        spread(lambda c: mine.at[c], lambda k: come.at[k - 1], s1, r1)
+
+    def cores():
+        pltpu.make_async_copy(come, come, r1).wait()
+        terms = [mine[me]] + [come[k] for k in range(chips - 1)]
+        while len(terms) > 1:
+            terms = [sum(terms[k : k + 2][1:], terms[k]) for k in range(0, len(terms), 2)]
+        part[...] = terms[0]
+        other.start()
+
+    def join():
+        other.wait_recv()
+        piece[...] = (part[...] + pair[...]) * factor
+        whole[me] = piece[...]
+        spread(lambda c: piece, lambda k: whole.at[me], s3, r3)
+
+    def finish():
+        pltpu.make_async_copy(whole.at[many], whole.at[many], r3).wait()
+        for c in range(chips):
+            out_ref[spots[c]] = whole[c]
+        pltpu.make_async_copy(come, come, s1).wait()
+        other.wait_send()
+        pltpu.make_async_copy(whole.at[many], whole.at[many], s3).wait()
+
+    return split, cores, join, finish
+
+
 def column_order(cols, early, order_ref):
     parts, picks = cols.shape
     count = parts * picks
@@ -221,14 +294,21 @@
         load.start()
 
     barrier = pltpu.get_barrier_semaphore()
-    for n in range(slabs - 1):
-        pl.semaphore_signal(barrier, inc=1, device_id={"grp": rec_peer(n)}, device_id_type=MESH)
-    for n in range(parts - 1):
-        pl.semaphore_signal(barrier, inc=1, device_id={"blk": lax.rem(b + n + 1, parts)}, device_id_type=MESH)
+    chips = parts * slabs // 2
+
+    def greet(k, _):
+        pb, pq, same = chip_peer(parts, slabs, k)
+        pl.semaphore_signal(barrier, inc=1, device_id={"blk": pb, "grp": pq * 2 + same}, device_id_type=MESH)
+        return 0
+
+    lax.fori_loop(1, chips, greet, 0)
+    for n in range(slabs // 2):
+        peer = (g // 2 + n) % (slabs // 2) * 2 + 1 - core
+        pl.semaphore_signal(barrier, inc=1, device_id={"grp": peer}, device_id_type=MESH)
 
     index_tables(slab_ref, local_ref, remote_ref, weight_ref, pair_ref, ext_ref)
     load_grad.wait()
-    pl.semaphore_wait(barrier, slabs + parts - 2)
+    pl.semaphore_wait(barrier, chips - 1 + slabs // 2)
 
     def rec_copy(n):
         return pltpu.make_async_remote_copy(
@@ -431,12 +511,13 @@
     for m in (5, 8, 9, 10):
         copies[m].wait_recv()
     products(early_ref, 0, early)
+    count = len(sum_scratch(parts, slabs, width))
+    upd_sum = sum_stages(parts, slabs, factor, upd_ref, out_upd_ref, scratch[:count])
+    msg_sum = chip_stages(parts, slabs, factor, msg_ref, out_msg_ref, scratch[count:])
+    upd_sum[0]()
     for m in (11, 12, 13, 14, 15, 16):
         copies[m].wait_recv()
-    half = len(scratch) // 2
-    upd_sum = sum_stages(parts, slabs, factor, upd_ref, out_upd_ref, scratch[:half])
-    msg_sum = sum_stages(parts, slabs, factor, msg_ref, out_msg_ref, scratch[half:])
-    upd_sum[0]()
+    upd_sum[1]()
     products(late_ref, early, tiles - early)
     for m in range(len(copies)):
         copies[m].wait_send()
@@ -447,13 +528,12 @@
         return 0
 
     lax.fori_loop(0, panels, settle, 0)
-    upd_sum[1]()
+    upd_sum[2]()
     msg = jnp.zeros((width, width), F32)
     for k in range(nodes // 256):
         msg += jnp.dot(turned_ref[k], gp_ref[2 * k : 2 * k + 2].reshape(256, width), preferred_element_type=F32)
     msg_ref[...] = msg
     msg_sum[0]()
-    upd_sum[2]()
 
     def features(i, _):
         at = pl.ds(pl.multiple_of(i * 512, 512), 512)
@@ -470,7 +550,6 @@
     msg_sum[2]()
     msg_sum[3]()
     upd_sum[4]()
-    msg_sum[4]()
     store_out.wait()
 
 
@@ -515,7 +594,8 @@
             pltpu.VMEM((width, width), F32),
             dma((3,)), dma((parts,)), dma((slabs - 1,)), dma((slabs,)), dma((17,)), dma((17,)), dma((2,)),
         ]
-        + sum_scratch(parts, slabs, width) * 2,
+        + sum_scratch(parts, slabs, width)
+        + chip_scratch(parts, slabs),
         compiler_params=pltpu.CompilerParams(collective_id=0, has_side_effects=True, vmem_limit_bytes=VMEM_LIMIT),
         name="main_step",
     )(picks, slab, local, remote, weight, cols, w_update, w_message, grad, pre, feats, tiles)

time: 185 us -> 183 us (0.989)
  Pallas kernels: 184 us -> 182 us
    pallas_call x1, Pallas kernels: 180 us -> 178 us  [main_step(): pl.pallas_call(functools.partial(main_kernel, parts, slabs, factor), out_...]
where the time goes in v10:
time: 183 us; the launch traced here: 182 us
  Pallas kernels  182 us (99%)
    pallas_call x1, Pallas kernels, main_step(): pl.pallas_call(functools.partial(main_kernel, parts, slabs, factor), out_...  178 us
    pallas_call x1, Pallas kernels, final_step(): pl.pallas_call(final_kernel, grid=(steps,), out_shape=[jax.ShapeDtypeStru...  3.94 us

profile of v10, /device:TPU:1, one launch (start us, length us, event | category | flops | bytes accessed | tf_op | source)
XLA Modules:
  0.0 182.5 jit_solution(13354868770558911456)
XLA Ops:
  0.6 177.9 %main_step.1 = (bf16[4096,256]{1,0:T(8,128)(2,1)}, f32[256,256]{1,0:T(8,128)}, f32[256,256]{1,0:T(8,128)}) custom-call(s32[8,8,16]{2,1,0:T(8,128)} %bitcast.15, s32[32,128]{1,0:T(8,128)} %bitcast.16, s32[32,128]{1,0:T(8,128)} %bitcast.17, s32[32,128]{1,0:T(8,128)} %bitcast.18, f32[32,128]{1,0:T(8,128)} %bitcast.19, s32[8,16]{1,0:T(8,128)} %bitcast.20, ...), custom_call_target="tpu_custom_call" | custom-call | tf_op jit(solution)/shard_map/main_step/pallas_call | solution.py:566
  178.5 3.9 %final_step.1 = (bf16[4096,256]{1,0:T(8,128)(2,1)}, f32[256,256]{1,0:T(8,128)}, f32[256,256]{1,0:T(8,128)}) custom-call(bf16[4096,256]{1,0:T(8,128)(2,1)} %get-tuple-element.9.out_ref, f32[256,256]{1,0:T(8,128)} %get-tuple-element.10.msg_ref, f32[256,256]{1,0:T(8,128)} %get-tuple-element.11.upd_ref), custom_call_target="tpu_custom_call" | custom-call | tf_op jit(solution)/shard_map/final_step/pallas_call | solution.py:614

commit v11 on v10

--- a/solution.py
+++ b/solution.py
@@ -294,21 +294,14 @@
         load.start()
 
     barrier = pltpu.get_barrier_semaphore()
-    chips = parts * slabs // 2
-
-    def greet(k, _):
-        pb, pq, same = chip_peer(parts, slabs, k)
-        pl.semaphore_signal(barrier, inc=1, device_id={"blk": pb, "grp": pq * 2 + same}, device_id_type=MESH)
-        return 0
-
-    lax.fori_loop(1, chips, greet, 0)
-    for n in range(slabs // 2):
-        peer = (g // 2 + n) % (slabs // 2) * 2 + 1 - core
-        pl.semaphore_signal(barrier, inc=1, device_id={"grp": peer}, device_id_type=MESH)
+    for n in range(slabs - 1):
+        pl.semaphore_signal(barrier, inc=1, device_id={"grp": rec_peer(n)}, device_id_type=MESH)
+    for n in range(parts - 1):
+        pl.semaphore_signal(barrier, inc=1, device_id={"blk": lax.rem(b + n + 1, parts)}, device_id_type=MESH)
 
     index_tables(slab_ref, local_ref, remote_ref, weight_ref, pair_ref, ext_ref)
     load_grad.wait()
-    pl.semaphore_wait(barrier, chips - 1 + slabs // 2)
+    pl.semaphore_wait(barrier, slabs + parts - 2)
 
     def rec_copy(n):
         return pltpu.make_async_remote_copy(
@@ -601,22 +594,33 @@
     )(picks, slab, local, remote, weight, cols, w_update, w_message, grad, pre, feats, tiles)
 
 
-def final_kernel(out_ref, msg_ref, upd_ref, to_out_ref, to_msg_ref, to_upd_ref):
-    to_out_ref[...] = out_ref[...]
-    to_msg_ref[...] = msg_ref[...]
-    to_upd_ref[...] = upd_ref[...]
+def final_kernel(out_ref, msg_ref, upd_ref, to_out_ref, to_msg_ref, to_upd_ref, out_buf, msg_buf, upd_buf, come, go):
+    steps = 4
+    rows = out_ref.shape[0] // steps
+    ways = [(msg_ref, msg_buf, to_msg_ref), (upd_ref, upd_buf, to_upd_ref)]
+    for k in range(steps):
+        at = pl.ds(k * rows, rows)
+        ways.append((out_ref.at[at], out_buf.at[at], to_out_ref.at[at]))
+    loads = [pltpu.make_async_copy(src, buf, come.at[k]) for k, (src, buf, _) in enumerate(ways)]
+    stores = [pltpu.make_async_copy(buf, dst, go.at[k]) for k, (_, buf, dst) in enumerate(ways)]
+    for load in loads:
+        load.start()
+    for load, store in zip(loads, stores):
+        load.wait()
+        store.start()
+    for store in stores:
+        store.wait()
 
 
 def final_step(out, msg, upd):
-    steps = 4
+    hbm = pl.BlockSpec(memory_space=pl.ANY)
     args = (out, msg, upd)
-    specs = [pl.BlockSpec((a.shape[0] // steps, a.shape[1]), lambda i: (i, 0)) for a in args]
     return pl.pallas_call(
         final_kernel,
-        grid=(steps,),
         out_shape=[jax.ShapeDtypeStruct(a.shape, a.dtype) for a in args],
-        in_specs=specs,
-        out_specs=specs,
+        in_specs=[hbm] * 3,
+        out_specs=[hbm] * 3,
+        scratch_shapes=[pltpu.VMEM(a.shape, a.dtype) for a in args] + [pltpu.SemaphoreType.DMA((6,))] * 2,
         compiler_params=pltpu.CompilerParams(vmem_limit_bytes=VMEM_LIMIT),
         name="final_step",
     )(*args)

time: 183 us -> 180 us (0.984)
  Pallas kernels: 182 us -> 179 us
where the time goes in v11:
time: 180 us; the launch traced here: 179 us
  Pallas kernels  179 us (99%)
    pallas_call x1, Pallas kernels, main_step(): pl.pallas_call(functools.partial(main_kernel, parts, slabs, factor), out_...  176 us

profile of v11, /device:TPU:1, one launch (start us, length us, event | category | flops | bytes accessed | tf_op | source)
XLA Modules:
  0.0 179.5 jit_solution(8777842035391862160)
XLA Ops:
  0.6 176.2 %main_step.1 = (bf16[4096,256]{1,0:T(8,128)(2,1)}, f32[256,256]{1,0:T(8,128)}, f32[256,256]{1,0:T(8,128)}) custom-call(s32[8,8,16]{2,1,0:T(8,128)} %bitcast.15, s32[32,128]{1,0:T(8,128)} %bitcast.16, s32[32,128]{1,0:T(8,128)} %bitcast.17, s32[32,128]{1,0:T(8,128)} %bitcast.18, f32[32,128]{1,0:T(8,128)} %bitcast.19, s32[8,16]{1,0:T(8,128)} %bitcast.20, ...), custom_call_target="tpu_custom_call" | custom-call | tf_op jit(solution)/shard_map/main_step/pallas_call | solution.py:559
  176.9 2.6 %final_step.1 = (bf16[4096,256]{1,0:T(8,128)(2,1)}, f32[256,256]{1,0:T(8,128)}, f32[256,256]{1,0:T(8,128)}) custom-call(bf16[4096,256]{1,0:T(8,128)(2,1)} %get-tuple-element.9.out_ref, f32[256,256]{1,0:T(8,128)} %get-tuple-element.10.msg_ref, f32[256,256]{1,0:T(8,128)} %get-tuple-element.11.upd_ref), custom_call_target="tpu_custom_call" | custom-call | tf_op jit(solution)/shard_map/final_step/pallas_call | solution.py:618

commit v12 on v11

--- a/solution.py
+++ b/solution.py
@@ -33,7 +33,7 @@
     totals = jnp.dot(flat16, jnp.ones((128, 128), BF16), preferred_element_type=F32)
     size = chunks * slabs
     row, col = iota((size, size), 0), iota((size, size), 1)
-    earlier = (col < row) & (lax.rem(col, slabs) == lax.rem(row, slabs))
+    earlier = (col < row) & (((col ^ row) & (slabs - 1)) == 0)
     offset = jnp.dot(jnp.where(earlier, 1.0, 0.0).astype(BF16), totals.astype(BF16), preferred_element_type=F32)
     place = ((prefix + offset) * flat).reshape(chunks, slabs, 128).sum(axis=1).astype(jnp.int32)
     remote, local, weight = remote_ref[...], local_ref[...], weight_ref[...]
@@ -51,9 +51,11 @@
         jnp.ones_like(weight),
     ]
     table = jnp.zeros((len(values) * slabs, cap), F32)
-    for c in range(chunks):
-        left = jnp.concatenate([choose[c] * v[c : c + 1] for v in values], axis=0).astype(BF16)
-        right = jnp.where(iota((cap, 128), 0) == place[c : c + 1], 1.0, 0.0).astype(BF16)
+    for c in range(0, chunks, 2):
+        pair = (c, c + 1)
+        left = [jnp.concatenate([choose[k] * v[k : k + 1] for v in values], axis=0).astype(BF16) for k in pair]
+        right = [jnp.where(iota((cap, 128), 0) == place[k : k + 1], 1.0, 0.0).astype(BF16) for k in pair]
+        left, right = jnp.concatenate(left, axis=1), jnp.concatenate(right, axis=1)
         table += lax.dot_general(left, right, NT, preferred_element_type=F32)
     valid = table[7 * slabs : 8 * slabs]
     upper_part = jnp.where(valid > 0.5, table[:slabs], 64.0)
@@ -409,7 +411,7 @@
             store(t, load(picks_ref[c, r, t]))
             return 0
 
-        lax.fori_loop(0, picks, one, 0)
+        lax.fori_loop(0, picks, one, 0, unroll=4)
 
     def to_stage(ref, n):
         def store(t, value):
@@ -462,7 +464,7 @@
         tiles_ref[k] = jnp.transpose(tiles_ref[k])
         return 0
 
-    lax.fori_loop(0, tiles, turn, 0)
+    lax.fori_loop(0, tiles, turn, 0, unroll=4)
     copies[6].wait_recv()
     copies[7].wait_recv()
     pack(to_stage(stage_a, 3), lambda i: far_ref[i], side, across)
@@ -520,7 +522,7 @@
         gp_ref[j] = (piece(j) + piece(j + panels)).astype(BF16)
         return 0
 
-    lax.fori_loop(0, panels, settle, 0)
+    lax.fori_loop(0, panels, settle, 0, unroll=4)
     upd_sum[2]()
     msg = jnp.zeros((width, width), F32)
     for k in range(nodes // 256):

time: 180 us -> 180 us (level)
  no operation moved by 1% of the time
where the time goes in v12:
time: 180 us
  Pallas kernels  179 us (99%)
    pallas_call x1, Pallas kernels, main_step(): pl.pallas_call(functools.partial(main_kernel, parts, slabs, factor), out_...  176 us

profile of v12, /device:TPU:1, one launch (start us, length us, event | category | flops | bytes accessed | tf_op | source)
XLA Modules:
  0.0 179.7 jit_solution(7668866103253390715)
XLA Ops:
  0.6 176.5 %main_step.1 = (bf16[4096,256]{1,0:T(8,128)(2,1)}, f32[256,256]{1,0:T(8,128)}, f32[256,256]{1,0:T(8,128)}) custom-call(s32[8,8,16]{2,1,0:T(8,128)} %bitcast.15, s32[32,128]{1,0:T(8,128)} %bitcast.16, s32[32,128]{1,0:T(8,128)} %bitcast.17, s32[32,128]{1,0:T(8,128)} %bitcast.18, f32[32,128]{1,0:T(8,128)} %bitcast.19, s32[8,16]{1,0:T(8,128)} %bitcast.20, ...), custom_call_target="tpu_custom_call" | custom-call | tf_op jit(solution)/shard_map/main_step/pallas_call | solution.py:561
  177.1 2.6 %final_step.1 = (bf16[4096,256]{1,0:T(8,128)(2,1)}, f32[256,256]{1,0:T(8,128)}, f32[256,256]{1,0:T(8,128)}) custom-call(bf16[4096,256]{1,0:T(8,128)(2,1)} %get-tuple-element.9.out_ref, f32[256,256]{1,0:T(8,128)} %get-tuple-element.10.msg_ref, f32[256,256]{1,0:T(8,128)} %get-tuple-element.11.upd_ref), custom_call_target="tpu_custom_call" | custom-call | tf_op jit(solution)/shard_map/final_step/pallas_call | solution.py:620

commit v13 on v11

--- a/solution.py
+++ b/solution.py
@@ -277,7 +277,7 @@
 
     def rec_peer(n):
         q = n // 4
-        dz, dx, dc = (n % 4 + 1) % 4, 1 - n // 8, (q + q // 2) % 2
+        dz, dx, dc = (2 + 3 * q + 3 * (q // 2) + 2 * (q // 3)) % 4, 1 - n % 4 // 2, 1 - n % 2
         return ((xl + dx) % 2 * 4 + (z + dz) % 4) * 2 + (core + dc) % 2
 
     ring = parts // 2
@@ -507,10 +507,9 @@
     count = len(sum_scratch(parts, slabs, width))
     upd_sum = sum_stages(parts, slabs, factor, upd_ref, out_upd_ref, scratch[:count])
     msg_sum = chip_stages(parts, slabs, factor, msg_ref, out_msg_ref, scratch[count:])
-    upd_sum[0]()
     for m in (11, 12, 13, 14, 15, 16):
         copies[m].wait_recv()
-    upd_sum[1]()
+    upd_sum[0]()
     products(late_ref, early, tiles - early)
     for m in range(len(copies)):
         copies[m].wait_send()
@@ -521,12 +520,12 @@
         return 0
 
     lax.fori_loop(0, panels, settle, 0)
-    upd_sum[2]()
     msg = jnp.zeros((width, width), F32)
     for k in range(nodes // 256):
         msg += jnp.dot(turned_ref[k], gp_ref[2 * k : 2 * k + 2].reshape(256, width), preferred_element_type=F32)
     msg_ref[...] = msg
     msg_sum[0]()
+    upd_sum[1]()
 
     def features(i, _):
         at = pl.ds(pl.multiple_of(i * 512, 512), 512)
@@ -539,8 +538,9 @@
     store_out = pltpu.make_async_copy(pre_ref, out_hbm, store_sem.at[1])
     store_out.start()
     msg_sum[1]()
+    upd_sum[2]()
+    msg_sum[2]()
     upd_sum[3]()
-    msg_sum[2]()
     msg_sum[3]()
     upd_sum[4]()
     store_out.wait()

time: 180 us -> 178 us (0.989)
  Pallas kernels: 179 us -> 177 us
    pallas_call x1, Pallas kernels: 176 us -> 174 us  [main_step(): pl.pallas_call(functools.partial(main_kernel, parts, slabs, factor), out_...]
where the time goes in v13:
time: 178 us; the launch traced here: 177 us
  Pallas kernels  177 us (99%)
    pallas_call x1, Pallas kernels, main_step(): pl.pallas_call(functools.partial(main_kernel, parts, slabs, factor), out_...  174 us

profile of v13, /device:TPU:1, one launch (start us, length us, event | category | flops | bytes accessed | tf_op | source)
XLA Modules:
  0.0 177.4 jit_solution(10124201186937207155)
XLA Ops:
  0.6 174.2 %main_step.1 = (bf16[4096,256]{1,0:T(8,128)(2,1)}, f32[256,256]{1,0:T(8,128)}, f32[256,256]{1,0:T(8,128)}) custom-call(s32[8,8,16]{2,1,0:T(8,128)} %bitcast.15, s32[32,128]{1,0:T(8,128)} %bitcast.16, s32[32,128]{1,0:T(8,128)} %bitcast.17, s32[32,128]{1,0:T(8,128)} %bitcast.18, f32[32,128]{1,0:T(8,128)} %bitcast.19, s32[8,16]{1,0:T(8,128)} %bitcast.20, ...), custom_call_target="tpu_custom_call" | custom-call | tf_op jit(solution)/shard_map/main_step/pallas_call | solution.py:559
  174.8 2.6 %final_step.1 = (bf16[4096,256]{1,0:T(8,128)(2,1)}, f32[256,256]{1,0:T(8,128)}, f32[256,256]{1,0:T(8,128)}) custom-call(bf16[4096,256]{1,0:T(8,128)(2,1)} %get-tuple-element.9.out_ref, f32[256,256]{1,0:T(8,128)} %get-tuple-element.10.msg_ref, f32[256,256]{1,0:T(8,128)} %get-tuple-element.11.upd_ref), custom_call_target="tpu_custom_call" | custom-call | tf_op jit(solution)/shard_map/final_step/pallas_call | solution.py:618
